TPU v7x, 32 devices: a whole 2x2x4 slice. The times are simulated.
32 devices in a mesh: dp: 16 (over z, x, core), tensor: 2 (over y).
Axes of the slice: x: 2, y: 2, z: 4, core: 2. Of those that a mesh axis runs over, the one named last changes fastest.
Arguments:
- residual: float32 [4096, 1024], P(('dp', 'tensor')), may hold values from -6 to 6
- out_grad: float32 [4096, 1024], P(('dp', 'tensor')), may hold values from -6 to 6
- doc_lengths: int32 [16, 4], P('dp'), may hold values from 0 to 256, as said below
- mixer_weight: float32 [1024, 3840], P('dp', 'tensor'), may hold values from -0.1875 to 0.1875
- mixer_first: float32 [1024, 3840], P('dp', 'tensor'), may hold values from -40 to 40
- mixer_second: float32 [1024, 3840], P('dp', 'tensor'), may hold values from 102.4 to 1638.4
- scan_weight: float32 [1024, 280], P('dp'), may hold values from -0.1875 to 0.1875
- scan_first: float32 [1024, 280], P('dp'), may hold values from -40 to 40
- scan_second: float32 [1024, 280], P('dp'), may hold values from 102.4 to 1638.4
- merge_weight: float32 [2048, 1024], P('tensor', 'dp'), may hold values from -0.25 to 0.25
- merge_first: float32 [2048, 1024], P('tensor', 'dp'), may hold values from -40 to 40
- merge_second: float32 [2048, 1024], P('tensor', 'dp'), may hold values from 102.4 to 1638.4
- hidden_weight: float32 [1024, 4096], P('dp', 'tensor'), may hold values from -0.1875 to 0.1875
- hidden_first: float32 [1024, 4096], P('dp', 'tensor'), may hold values from -40 to 40
- hidden_second: float32 [1024, 4096], P('dp', 'tensor'), may hold values from 102.4 to 1638.4
- down_weight: float32 [2048, 1024], P('tensor', 'dp'), may hold values from -0.125 to 0.125
- down_first: float32 [2048, 1024], P('tensor', 'dp'), may hold values from -40 to 40
- down_second: float32 [2048, 1024], P('tensor', 'dp'), may hold values from 102.4 to 1638.4
- head_params: float32 [24, 323], P('tensor'), may hold values from -4 to 1.5, as said below
- head_first: float32 [24, 323], P('tensor'), may hold values from -40 to 40
- head_second: float32 [24, 323], P('tensor'), may hold values from 102.4 to 1638.4
- shared_params: float32 [3328], replicated, may hold values from -1.5 to 1.5, as said below
- shared_first: float32 [3328], replicated, may hold values from -40 to 40
- shared_second: float32 [3328], replicated, may hold values from 102.4 to 1638.4
Outputs:
- block_out: float32 [4096, 1024], P(('dp', 'tensor'))
- input_grad: float32 [4096, 1024], P(('dp', 'tensor'))
- mixer_momentum: float32 [1024, 3840], P('dp', 'tensor')
- mixer_squares: float32 [1024, 3840], P('dp', 'tensor')
- mixer_updated: float32 [1024, 3840], P('dp', 'tensor')
- scan_momentum: float32 [1024, 280], P('dp')
- scan_squares: float32 [1024, 280], P('dp')
- scan_updated: float32 [1024, 280], P('dp')
- merge_momentum: float32 [2048, 1024], P('tensor', 'dp')
- merge_squares: float32 [2048, 1024], P('tensor', 'dp')
- merge_updated: float32 [2048, 1024], P('tensor', 'dp')
- hidden_momentum: float32 [1024, 4096], P('dp', 'tensor')
- hidden_squares: float32 [1024, 4096], P('dp', 'tensor')
- hidden_updated: float32 [1024, 4096], P('dp', 'tensor')
- down_momentum: float32 [2048, 1024], P('tensor', 'dp')
- down_squares: float32 [2048, 1024], P('tensor', 'dp')
- down_updated: float32 [2048, 1024], P('tensor', 'dp')
- head_momentum: float32 [24, 323], P('tensor')
- head_squares: float32 [24, 323], P('tensor')
- head_updated: float32 [24, 323], P('tensor')
- shared_momentum: float32 [3328], replicated
- shared_squares: float32 [3328], replicated
- shared_updated: float32 [3328], replicated
Inputs may be any that keep to these rules, and one draw needn't show every extreme that they name: `doc_lengths`: each row lists the lengths of the documents of one group in order and sums to 256; zeros are empty slots. The first document of each row is longer than half of 256; one row holds a single document of 256 tokens. `head_params`: columns below 256: convolution taps; next 64: biases; then a_log, skip, dt_bias. `shared_params`: gains first, then taps, then biases.
All inputs are finite; a program needn't handle non-finite values.
Results may differ from a plain program's by a relative error of at most 0.012.
The roundings to bfloat16 on the way count: a program that leaves them out, or rounds other values in their place, can miss the bound.
Values may be sent and summed in bfloat16 or wider, within the bound.
No kernel may reach another device: no remote copies, remote signals or barrier semaphores. Data moves between devices by JAX's collectives and lax.ppermute only.
A program may use at most 128 MiB of HBM per device.

v0:
```python
import jax
import jax.numpy as jnp
from jax import lax
from jax.sharding import PartitionSpec as P

D = 1024
HEADS_M = 24
HEAD_M = 64
STATE = 128
CONV = 4
HEADS_Q = 8
HEADS_KV = 2
HEAD_A = 64
STEP = 10


EPS = 1e-05
THETA = 10000.0
HIGH = lax.Precision.HIGHEST


def scaled_norm(values, gain):
    return values * lax.rsqrt(jnp.mean(values * values, axis=-1, keepdims=True) + EPS) * gain


def doc_index(lens, count):
    place = jnp.arange(count, dtype=jnp.int32)
    ends = jnp.cumsum(lens)
    after = place[:, None] >= ends[None, :]
    seg = jnp.sum(after.astype(jnp.int32), axis=1)
    start = jnp.sum(jnp.where(after, lens[None, :], 0), axis=1)
    return (seg, place - start)


def causal_conv(values, taps, bias, seg):
    length = values.shape[0]
    total = bias[None, :] + taps[CONV - 1][None, :] * values
    for shift in range(1, CONV):
        moved = jnp.pad(values, ((shift, 0), (0, 0)))[:length]
        keep = jnp.pad(seg, (shift, 0), constant_values=-1)[:length] == seg
        total = total + taps[CONV - 1 - shift][None, :] * jnp.where(keep[:, None], moved, 0.0)
    return total


def rotate(values, pos):
    half = HEAD_A // 2
    freq = THETA ** (-jnp.arange(half, dtype=jnp.float32) * 2.0 / HEAD_A)
    angle = pos.astype(jnp.float32)[:, None] * freq[None, :]
    cosine = jnp.cos(angle)[:, None, :]
    sine = jnp.sin(angle)[:, None, :]
    first = values[..., :half]
    second = values[..., half:]
    return jnp.concatenate(
        [first * cosine - second * sine, second * cosine + first * sine], axis=-1
    )


def mixer(pmat, scan, heads, conv_shared, seg, pos, tpos):
    length = pmat.shape[0]
    count = heads.shape[0]
    width = count * HEAD_M
    qheads = HEADS_Q * count // HEADS_M
    kheads = HEADS_KV * count // HEADS_M
    gates = pmat[:, :width]
    chans = pmat[:, width : 2 * width]
    qpart = pmat[:, 2 * width : 2 * width + qheads * HEAD_A]
    kpart = pmat[:, 2 * width + qheads * HEAD_A : 2 * width + (qheads + kheads) * HEAD_A]
    vpart = pmat[
        :, 2 * width + (qheads + kheads) * HEAD_A : 2 * width + (qheads + 2 * kheads) * HEAD_A
    ]
    taps = jnp.stack([heads[:, k * HEAD_M : (k + 1) * HEAD_M].reshape(-1) for k in range(CONV)])
    bias = heads[:, CONV * HEAD_M : (CONV + 1) * HEAD_M].reshape(-1)
    conv_chans = jax.nn.silu(causal_conv(chans, taps, bias, seg))
    states = jax.nn.silu(
        causal_conv(scan[:, : 2 * STATE], conv_shared[:CONV], conv_shared[CONV], seg)
    )
    in_state = states[:, :STATE]
    out_state = states[:, STATE:]
    base = (CONV + 1) * HEAD_M
    rates = jnp.exp(heads[:, base])
    skip = heads[:, base + 1]
    dt_bias = heads[:, base + 2]
    step_raw = lax.dynamic_slice_in_dim(scan, 2 * STATE + tpos * count, count, 1)
    steps = jax.nn.softplus(step_raw + dt_bias[None, :])
    cum = jnp.cumsum(-rates[None, :] * steps, axis=0)
    place = jnp.arange(length, dtype=jnp.int32)
    same = (seg[:, None] == seg[None, :]) & (place[:, None] >= place[None, :])
    gap = cum.T[:, :, None] - cum.T[:, None, :]
    decay = jnp.where(same[None], jnp.exp(jnp.where(same[None], gap, 0.0)), 0.0)
    inner = jnp.dot(out_state, in_state.T, precision=HIGH)
    heads_x = conv_chans.reshape(length, count, HEAD_M)
    weighted = heads_x * steps[:, :, None]
    outputs = jnp.einsum("hts,shp->thp", decay * inner[None], weighted, precision=HIGH)
    outputs = outputs + skip[None, :, None] * heads_x
    outputs = outputs * jax.nn.silu(gates.reshape(length, count, HEAD_M))
    query = rotate(qpart.reshape(length, qheads, HEAD_A), pos).reshape(
        length, kheads, qheads // kheads, HEAD_A
    )
    keys = rotate(kpart.reshape(length, kheads, HEAD_A), pos)
    vals = vpart.reshape(length, kheads, HEAD_A)
    scores = jnp.einsum("tkgd,skd->kgts", query, keys, precision=HIGH) * HEAD_A ** (-0.5)
    scores = jnp.where(same[None, None], scores, -1e30)
    probs = jax.nn.softmax(scores, axis=-1)
    attended = jnp.einsum("kgts,skd->tkgd", probs, vals, precision=HIGH).reshape(
        length, qheads * HEAD_A
    )
    return jnp.concatenate([outputs.reshape(length, width), attended], axis=1)


def swiglu(gate, upper):
    return jax.nn.silu(gate) * upper


def cross(left, right):
    return lax.dot_general(
        left, right, (((0,), (0,)), ((), ())), preferred_element_type=jnp.float32
    )


def back_dot(grad, weight):
    return lax.dot_general(
        grad, weight, (((1,), (1,)), ((), ())), preferred_element_type=jnp.float32
    )


def adamw(weight, first, second, grad, rate, decay):
    first = 0.9 * first + 0.1 * grad
    second = 0.95 * second + 0.05 * grad * grad
    fixed_one = first / (1.0 - 0.9**STEP)
    fixed_two = second / (1.0 - 0.95**STEP)
    weight = weight - rate * (fixed_one / (jnp.sqrt(fixed_two) + 1e-08) + decay * weight)
    return (first, second, weight)


def per_device(
    residual,
    out_grad,
    doc_lengths,
    mixer_weight,
    mixer_first,
    mixer_second,
    scan_weight,
    scan_first,
    scan_second,
    merge_weight,
    merge_first,
    merge_second,
    hidden_weight,
    hidden_first,
    hidden_second,
    down_weight,
    down_first,
    down_second,
    head_params,
    head_first,
    head_second,
    shared_params,
    shared_first,
    shared_second,
):
    tidx = lax.axis_index("tensor")
    group = residual.shape[0] * lax.axis_size("tensor")
    seg, pos = doc_index(doc_lengths[0], group)
    gain_one = shared_params[:D]
    gain_two = shared_params[D : 2 * D]
    conv_shared = shared_params[2 * D :].reshape(CONV + 1, 2 * STATE)
    lowered = (
        mixer_weight.astype(jnp.bfloat16),
        scan_weight.astype(jnp.bfloat16),
        hidden_weight.astype(jnp.bfloat16),
        merge_weight.astype(jnp.bfloat16),
        down_weight.astype(jnp.bfloat16),
    )
    mix_full, scan_full, hidden_full, merge_full, down_full = (
        lax.all_gather(lowered[0], "dp", axis=0, tiled=True),
        lax.all_gather(lowered[1], "dp", axis=0, tiled=True),
        lax.all_gather(lowered[2], "dp", axis=0, tiled=True),
        lax.all_gather(lowered[3], "dp", axis=1, tiled=True),
        lax.all_gather(lowered[4], "dp", axis=1, tiled=True),
    )
    normed_one, norm_back_one = jax.vjp(scaled_norm, residual, gain_one)
    first_in = normed_one.astype(jnp.bfloat16)
    scan_own = jnp.dot(first_in, scan_full, preferred_element_type=jnp.float32).astype(jnp.bfloat16)
    first_all, scan_all = (
        lax.all_gather(first_in, "tensor", axis=0, tiled=True),
        lax.all_gather(scan_own, "tensor", axis=0, tiled=True),
    )
    projected = jnp.dot(first_all, mix_full, preferred_element_type=jnp.float32).astype(
        jnp.bfloat16
    )

    def mixer_local(pmat, scan, heads, conv):
        return mixer(pmat, scan, heads, conv, seg, pos, tidx)

    proj_wide = projected.astype(jnp.float32)
    scan_wide = scan_all.astype(jnp.float32)
    joined, mixer_back = jax.vjp(mixer_local, proj_wide, scan_wide, head_params, conv_shared)
    joined_low = joined.astype(jnp.bfloat16)
    merged = lax.psum_scatter(
        jnp.dot(joined_low, merge_full, preferred_element_type=jnp.float32),
        "tensor",
        scatter_dimension=0,
        tiled=True,
    )
    middle = residual + merged
    normed_two, norm_back_two = jax.vjp(scaled_norm, middle, gain_two)
    second_in = normed_two.astype(jnp.bfloat16)
    second_all = lax.all_gather(second_in, "tensor", axis=0, tiled=True)
    gate_up = jnp.dot(second_all, hidden_full, preferred_element_type=jnp.float32)
    units = gate_up.shape[1] // 2
    activ, swiglu_back = jax.vjp(swiglu, gate_up[:, :units], gate_up[:, units:])
    activ_low = activ.astype(jnp.bfloat16)
    feed = lax.psum_scatter(
        jnp.dot(activ_low, down_full, preferred_element_type=jnp.float32).astype(jnp.bfloat16),
        "tensor",
        scatter_dimension=0,
        tiled=True,
    ).astype(jnp.float32)
    block_out = middle + feed
    back_mix, back_scan, back_hidden, back_merge, back_down = (
        lax.all_gather(lowered[0], "dp", axis=0, tiled=True),
        lax.all_gather(lowered[1], "dp", axis=0, tiled=True),
        lax.all_gather(lowered[2], "dp", axis=0, tiled=True),
        lax.all_gather(lowered[3], "dp", axis=1, tiled=True),
        lax.all_gather(lowered[4], "dp", axis=1, tiled=True),
    )
    grad_feed = lax.all_gather(out_grad.astype(jnp.bfloat16), "tensor", axis=0, tiled=True)
    down_grad = cross(activ_low, grad_feed)
    grad_activ = back_dot(grad_feed, back_down)
    grad_gate, grad_upper = swiglu_back(grad_activ)
    grad_gu = jnp.concatenate([grad_gate, grad_upper], axis=1).astype(jnp.bfloat16)
    hidden_grad = cross(second_all, grad_gu)
    grad_second = lax.psum_scatter(
        back_dot(grad_gu, back_hidden), "tensor", scatter_dimension=0, tiled=True
    )
    grad_middle_part, gain_two_grad = norm_back_two(grad_second)
    grad_middle = out_grad + grad_middle_part
    grad_mixed = lax.all_gather(grad_middle.astype(jnp.bfloat16), "tensor", axis=0, tiled=True)
    merge_grad = cross(joined_low, grad_mixed)
    grad_joined = back_dot(grad_mixed, back_merge)
    grad_proj, grad_scan, head_grad, conv_grad = mixer_back(grad_joined)
    grad_proj_low = grad_proj.astype(jnp.bfloat16)
    mixer_grad = cross(first_all, grad_proj_low)
    grad_first_part, grad_scan_own = (
        lax.psum_scatter(
            back_dot(grad_proj_low, back_mix), "tensor", scatter_dimension=0, tiled=True
        ),
        lax.psum_scatter(grad_scan, "tensor", scatter_dimension=0, tiled=True),
    )
    grad_scan_low = grad_scan_own.astype(jnp.bfloat16)
    scan_grad = cross(first_in, grad_scan_low)
    grad_first = grad_first_part + back_dot(grad_scan_low, back_scan)
    grad_resid_part, gain_one_grad = norm_back_one(grad_first)
    input_grad = grad_middle + grad_resid_part
    mixer_sum, hidden_sum, merge_sum, down_sum = (
        lax.psum_scatter(mixer_grad, "dp", scatter_dimension=0, tiled=True),
        lax.psum_scatter(hidden_grad, "dp", scatter_dimension=0, tiled=True),
        lax.psum_scatter(merge_grad, "dp", scatter_dimension=1, tiled=True),
        lax.psum_scatter(down_grad, "dp", scatter_dimension=1, tiled=True),
    )
    head_rows = head_grad.shape[0]
    heads_full = lax.dynamic_update_slice_in_dim(
        jnp.zeros((HEADS_M, head_grad.shape[1]), jnp.float32), head_grad, tidx * head_rows, 0
    )
    shared_grad = jnp.concatenate([gain_one_grad, gain_two_grad, conv_grad.reshape(-1)])
    shared_sum, heads_sum, scan_sum = lax.psum(
        (shared_grad, heads_full, scan_grad), ("dp", "tensor")
    )
    head_sum = lax.dynamic_slice_in_dim(heads_sum, tidx * head_rows, head_rows, 0)
    scan_rows = scan_weight.shape[0]
    scan_own_grad = lax.dynamic_slice_in_dim(
        scan_sum, lax.axis_index("dp") * scan_rows, scan_rows, 0
    )
    mixer_new = adamw(mixer_weight, mixer_first, mixer_second, mixer_sum, 0.02, 0.1)
    scan_new = adamw(scan_weight, scan_first, scan_second, scan_own_grad, 0.02, 0.1)
    merge_new = adamw(merge_weight, merge_first, merge_second, merge_sum, 0.02, 0.1)
    hidden_new = adamw(hidden_weight, hidden_first, hidden_second, hidden_sum, 0.02, 0.1)
    down_new = adamw(down_weight, down_first, down_second, down_sum, 0.02, 0.1)
    head_new = adamw(head_params, head_first, head_second, head_sum, 0.2, 0.0)
    shared_new = adamw(shared_params, shared_first, shared_second, shared_sum, 0.2, 0.0)
    return (
        block_out,
        input_grad,
        mixer_new[0],
        mixer_new[1],
        mixer_new[2],
        scan_new[0],
        scan_new[1],
        scan_new[2],
        merge_new[0],
        merge_new[1],
        merge_new[2],
        hidden_new[0],
        hidden_new[1],
        hidden_new[2],
        down_new[0],
        down_new[1],
        down_new[2],
        head_new[0],
        head_new[1],
        head_new[2],
        shared_new[0],
        shared_new[1],
        shared_new[2],
    )


def solution(mesh):
    return jax.shard_map(
        per_device,
        mesh=mesh,
        in_specs=(
            P(("dp", "tensor"), None),
            P(("dp", "tensor"), None),
            P("dp", None),
            P("dp", "tensor"),
            P("dp", "tensor"),
            P("dp", "tensor"),
            P("dp", None),
            P("dp", None),
            P("dp", None),
            P("tensor", "dp"),
            P("tensor", "dp"),
            P("tensor", "dp"),
            P("dp", "tensor"),
            P("dp", "tensor"),
            P("dp", "tensor"),
            P("tensor", "dp"),
            P("tensor", "dp"),
            P("tensor", "dp"),
            P("tensor", None),
            P("tensor", None),
            P("tensor", None),
            P(),
            P(),
            P(),
        ),
        out_specs=(
            P(("dp", "tensor"), None),
            P(("dp", "tensor"), None),
            P("dp", "tensor"),
            P("dp", "tensor"),
            P("dp", "tensor"),
            P("dp", None),
            P("dp", None),
            P("dp", None),
            P("tensor", "dp"),
            P("tensor", "dp"),
            P("tensor", "dp"),
            P("dp", "tensor"),
            P("dp", "tensor"),
            P("dp", "tensor"),
            P("tensor", "dp"),
            P("tensor", "dp"),
            P("tensor", "dp"),
            P("tensor", None),
            P("tensor", None),
            P("tensor", None),
            P(),
            P(),
            P(),
        ),
        check_vma=False,
    )
```

profile of v0, /device:TPU:0, one launch (start us, length us, event | category | flops | bytes accessed | tf_op | source)
XLA Modules:
  0.0 858.3 jit_solution(7323281332325516430)
XLA Ops:
  15.2 9.9 %all_gather.35 = bf16[256,1024]{1,0:T(8,128)(2,1)S(1)} all-gather(bf16[128,1024]{1,0:T(8,128)(2,1)S(1)} %multiply_convert_fusion.4), channel_id=1, replica_groups=mesh['dp'=16,'tensor'=2] {'tensor'}, dimensions={0}, use_global_device_ids=true | all-gather | bytes 786432 | tf_op jit(solution)/shard_map/all_gather | solution.py:185
  25.6 26.3 %all_gather.37 = bf16[1024,280]{1,0:T(8,128)(2,1)S(1)} all-gather(bf16[64,280]{1,0:T(8,128)(2,1)S(1)} %convert_element_type.84), channel_id=1, replica_groups=mesh['dp'=16,'tensor'=2] {'dp'}, dimensions={0}, use_global_device_ids=true | all-gather | bytes 609280 | tf_op jit(solution)/shard_map/all_gather | solution.py:176
  52.4 5.2 all_gather.38
  64.6 3.8 fusion.152
  76.9 4.7 multiply_convert_fusion.2
  81.6 25.6 %all-gather.7.cloned.1.call-done = bf16[1024,1024]{0,1:T(8,128)(2,1)} async-done(((bf16[1024,64]{0,1:T(8,128)(2,1)}), bf16[1024,1024]{0,1:T(8,128)(2,1)}) %all-gather.7.cloned.1.call-update) | async-done | bytes 2097168 | tf_op jit(solution)/shard_map/all_gather | solution.py:178
  107.2 3.4 fusion.69
  114.3 15.0 %all_gather.43 = bf16[256,1024]{1,0:T(8,128)(2,1)} all-gather(bf16[128,1024]{1,0:T(8,128)(2,1)S(1)} %convert_element_type.95), channel_id=1, replica_groups=mesh['dp'=16,'tensor'=2] {'tensor'}, dimensions={0}, use_global_device_ids=true | all-gather | bytes 786432 | tf_op jit(solution)/shard_map/all_gather | solution.py:227
  129.3 6.3 reduce-scatter.10.cloned.1.call-done
  136.8 9.1 %all_gather.40 = bf16[256,1024]{1,0:T(8,128)(2,1)} all-gather(bf16[128,1024]{1,0:T(8,128)(2,1)S(1)} %multiply_convert_fusion.3), channel_id=1, replica_groups=mesh['dp'=16,'tensor'=2] {'tensor'}, dimensions={0}, use_global_device_ids=true | all-gather | bytes 786432 | tf_op jit(solution)/shard_map/all_gather | solution.py:208
  145.9 42.1 %all-gather.9.cloned.1.call-done = bf16[1024,2048]{1,0:T(8,128)(2,1)} async-done(((bf16[64,2048]{1,0:T(8,128)(2,1)}), bf16[1024,2048]{1,0:T(8,128)(2,1)}) %all-gather.9.cloned.1.call-update) | async-done | bytes 4194320 | tf_op jit(solution)/shard_map/all_gather | solution.py:177
  188.0 4.9 fusion.154
  192.9 37.8 %all-gather.11.cloned.1.call-done = bf16[1024,1024]{0,1:T(8,128)(2,1)} async-done(((bf16[1024,64]{0,1:T(8,128)(2,1)}), bf16[1024,1024]{0,1:T(8,128)(2,1)}) %all-gather.11.cloned.1.call-update) | async-done | bytes 2097168 | tf_op jit(solution)/shard_map/all_gather | solution.py:179
  230.7 4.3 fusion.31
  238.4 3.3 convolution_convert_fusion.1
  242.4 15.2 %reduce-scatter.14.cloned.1.call-done = f32[128,1024]{1,0:T(8,128)} async-done(((f32[256,1024]{1,0:T(8,128)}), f32[128,1024]{1,0:T(8,128)}) %reduce-scatter.14.cloned.1.call-update) | async-done | bytes 524304 | tf_op jit(solution)/shard_map/reduce_scatter | solution.py:233
  259.3 15.6 %reduce-scatter.12.cloned.1.call-done = bf16[128,1024]{1,0:T(8,128)(2,1)} async-done(((bf16[256,1024]{1,0:T(8,128)(2,1)}), bf16[128,1024]{1,0:T(8,128)(2,1)}) %reduce-scatter.12.cloned.1.call-update) | async-done | bytes 262160 | tf_op jit(solution)/shard_map/reduce_scatter | solution.py:213
  277.5 8.7 %all_gather.44 = bf16[256,1024]{1,0:T(8,128)(2,1)S(1)} all-gather(bf16[128,1024]{1,0:T(8,128)(2,1)S(1)} %get-tuple-element.82), channel_id=1, replica_groups=mesh['dp'=16,'tensor'=2] {'tensor'}, dimensions={0}, use_global_device_ids=true | all-gather | bytes 786432 | tf_op jit(solution)/shard_map/all_gather | solution.py:238
  289.3 7.0 fusion.7
  307.2 5.5 multiply_add_fusion
  318.6 3.1 multiply_reduce_fusion.5
  323.0 6.4 reduce-scatter.18.cloned.1.call-done
  332.0 4.7 fusion.131
  344.8 4.6 fusion.60
  350.5 5.5 fusion.130
  358.4 109.2 %all-reduce.48.cloned.1.call-done = f32[1024,280]{1,0:T(8,128)} async-done(((f32[1024,280]{1,0:T(8,128)}), f32[1024,280]{1,0:T(8,128)}) %all-reduce.48.cloned.1.call-update) | async-done | bytes 1146896 | tf_op jit(solution)/shard_map/psum | solution.py:266
  469.2 19.8 %reduce-scatter.16.cloned.1.call-done = f32[128,1024]{1,0:T(8,128)} async-done(((f32[256,1024]{1,0:T(8,128)}), f32[128,1024]{1,0:T(8,128)}) %reduce-scatter.16.cloned.1.call-update) | async-done | bytes 524304 | tf_op jit(solution)/shard_map/reduce_scatter | solution.py:245
  490.5 40.1 %all-reduce.45 = (f32[24,323]{1,0:T(8,128)S(1)}, f32[3328]{0:T(1024)S(1)}) all-reduce(f32[24,323]{1,0:T(8,128)S(1)} %dynamic_update_slice.7, f32[3328]{0:T(1024)S(1)} %pad_maximum_fusion.9), channel_id=1, replica_groups=mesh['dp'=16,'tensor'=2] {'dp','tensor'}, use_global_device_ids=true, to_apply=%region_37.38 | all-reduce | flops 11080 | bytes 88640 | tf_op jit(solution)/shard_map/psum | solution.py:266
  532.9 33.2 %reduce-scatter.26.cloned.1.call-done = f32[1024,64]{0,1:T(8,128)} async-done(((f32[1024,1024]{0,1:T(8,128)}), f32[1024,64]{0,1:T(8,128)}) %reduce-scatter.26.cloned.1.call-update) | async-done | bytes 262160 | tf_op jit(solution)/shard_map/reduce_scatter | solution.py:259
  568.1 73.9 %reduce-scatter.22.cloned.1.call-done = f32[1024,64]{0,1:T(8,128)} async-done(((f32[1024,1024]{0,1:T(8,128)}), f32[1024,64]{0,1:T(8,128)}) %reduce-scatter.22.cloned.1.call-update) | async-done | bytes 262160 | tf_op jit(solution)/shard_map/reduce_scatter | solution.py:258
  644.1 105.6 %reduce-scatter.24.cloned.1.call-done = f32[64,2048]{1,0:T(8,128)} async-done(((f32[1024,2048]{1,0:T(8,128)}), f32[64,2048]{1,0:T(8,128)}) %reduce-scatter.24.cloned.1.call-update) | async-done | bytes 524304 | tf_op jit(solution)/shard_map/reduce_scatter | solution.py:257
  752.2 96.7 %reduce-scatter.20.cloned.1.call-done = f32[64,1920]{1,0:T(8,128)} async-done(((f32[1024,1920]{1,0:T(8,128)}), f32[64,1920]{1,0:T(8,128)}) %reduce-scatter.20.cloned.1.call-update) | async-done | bytes 491536 | tf_op jit(solution)/shard_map/reduce_scatter | solution.py:256
  (446 shorter events, 85.7 us)
Async XLA Ops:
  7.2 57.4 %all-gather.5.cloned.1.call-start = ((), (), s32[]{:S(2)}) async-start(), calls=%async_computation.9 | async-start | bytes 4177920 | tf_op jit(solution)/shard_map/all_gather | solution.py:175
  9.1 98.1 %all-gather.7.cloned.1.call-start = ((), (), s32[]{:S(2)}) async-start(), calls=%async_computation.10 | async-start | bytes 2228224 | tf_op jit(solution)/shard_map/all_gather | solution.py:178
  10.8 124.7 %reduce-scatter.10.cloned.1.call-start = ((), (), s32[]{:S(2)}) async-start(), calls=%async_computation.11 | async-start | bytes 1572864 | tf_op jit(solution)/shard_map/reduce_scatter | solution.py:199
  110.7 77.3 %all-gather.9.cloned.1.call-start = ((), (), s32[]{:S(2)}) async-start(), calls=%async_computation.12 | async-start | bytes 4456448 | tf_op jit(solution)/shard_map/all_gather | solution.py:177
  111.5 119.3 %all-gather.11.cloned.1.call-start = ((), (), s32[]{:S(2)}) async-start(), calls=%async_computation.13 | async-start | bytes 2228224 | tf_op jit(solution)/shard_map/all_gather | solution.py:179
  113.2 144.4 %reduce-scatter.14.cloned.1.call-start = ((), (), s32[]{:S(2)}) async-start(), calls=%async_computation.15 | async-start | bytes 1572864 | tf_op jit(solution)/shard_map/reduce_scatter | solution.py:233
  238.3 36.6 %reduce-scatter.12.cloned.1.call-start = ((), (), s32[]{:S(2)}) async-start(), calls=%async_computation.14 | async-start | bytes 786432 | tf_op jit(solution)/shard_map/reduce_scatter | solution.py:213
  241.7 87.7 %reduce-scatter.18.cloned.1.call-start = ((), (), s32[]{:S(2)}) async-start(), calls=%async_computation.17 | async-start | bytes 430080 | tf_op jit(solution)/shard_map/reduce_scatter | solution.py:248
  317.2 150.3 %all-reduce.48.cloned.1.call-start = ((), (), s32[]{:S(2)}) async-start(), calls=%async_computation.19 | async-start | bytes 3145728 | tf_op jit(solution)/shard_map/psum | solution.py:266
  331.9 157.1 %reduce-scatter.16.cloned.1.call-start = ((), (), s32[]{:S(2)}) async-start(), calls=%async_computation.16 | async-start | bytes 1572864 | tf_op jit(solution)/shard_map/reduce_scatter | solution.py:245
  336.7 229.4 %reduce-scatter.26.cloned.1.call-start = ((), (), s32[]{:S(2)}) async-start(), calls=%async_computation.22 | async-start | bytes 4456448 | tf_op jit(solution)/shard_map/reduce_scatter | solution.py:259
  339.6 302.5 %reduce-scatter.22.cloned.1.call-start = ((), (), s32[]{:S(2)}) async-start(), calls=%async_computation.20 | async-start | bytes 4456448 | tf_op jit(solution)/shard_map/reduce_scatter | solution.py:258
  343.5 406.3 %reduce-scatter.24.cloned.1.call-start = ((), (), s32[]{:S(2)}) async-start(), calls=%async_computation.21 | async-start | bytes 8912896 | tf_op jit(solution)/shard_map/reduce_scatter | solution.py:257
  349.5 499.5 %reduce-scatter.20.cloned.1.call-start = ((), (), s32[]{:S(2)}) async-start(), calls=%async_computation.18 | async-start | bytes 8355840 | tf_op jit(solution)/shard_map/reduce_scatter | solution.py:256
  356.1 132.9 %copy-start.41 = (f32[128,280]{0,1:T(8,128)S(1)}, f32[128,280]{0,1:T(8,128)}, u32[]{:S(2)}) copy-start(f32[128,280]{0,1:T(8,128)} %reduce-scatter.18.cloned.1.call-done) | copy-start | bytes 430084
  356.1 132.9 %copy-start.121 = (f32[128]{0:T(128)S(1)}, f32[128]{0:T(128)}, u32[]{:S(2)}) copy-start(f32[128]{0:T(128)} %copy-done.120) | copy-start | bytes 1540
  356.1 132.8 %copy-start.3 = (bf16[1024,280]{1,0:T(8,128)(2,1)S(1)}, bf16[1024,280]{1,0:T(8,128)(2,1)}, u32[]{:S(2)}) copy-start(bf16[1024,280]{1,0:T(8,128)(2,1)} %copy-done.2) | copy-start | bytes 1720324
  356.8 133.7 %copy-start.100 = (f32[1024]{0:T(1024)S(1)}, f32[1024]{0:T(1024)}, u32[]{:S(2)}) copy-start(f32[1024]{0:T(1024)} %get-tuple-element.33) | copy-start | bytes 12292
  357.0 173.6 %copy-start.131 = (f32[128]{0:T(128)S(1)}, f32[128]{0:T(128)}, u32[]{:S(2)}) copy-start(f32[128]{0:T(128)} %copy-done.130) | copy-start | bytes 1540
  357.0 173.6 %copy-start.77 = (f32[3328]{0:T(1024)S(1)}, f32[3328]{0:T(1024)}, u32[]{:S(2)}) copy-start(f32[3328]{0:T(1024)} %param.45) | copy-start | bytes 39940
  357.0 173.7 %copy-start.101 = (f32[3328]{0:T(1024)S(1)}, f32[3328]{0:T(1024)}, u32[]{:S(2)}) copy-start(f32[3328]{0:T(1024)} %param.47) | copy-start | bytes 39940
  357.0 173.7 %copy-start.102 = (f32[3328]{0:T(1024)S(1)}, f32[3328]{0:T(1024)}, u32[]{:S(2)}) copy-start(f32[3328]{0:T(1024)} %param.46) | copy-start | bytes 39940
  357.3 174.0 %copy-start.54 = (f32[12,323]{1,0:T(8,128)S(1)}, f32[12,323]{1,0:T(8,128)}, u32[]{:S(2)}) copy-start(f32[12,323]{1,0:T(8,128)} %param.42) | copy-start | bytes 46516
  357.3 174.0 %copy-start.95 = (f32[12,323]{1,0:T(8,128)S(1)}, f32[12,323]{1,0:T(8,128)}, u32[]{:S(2)}) copy-start(f32[12,323]{1,0:T(8,128)} %param.44) | copy-start | bytes 46516
  357.3 174.0 %copy-start.96 = (f32[12,323]{1,0:T(8,128)S(1)}, f32[12,323]{1,0:T(8,128)}, u32[]{:S(2)}) copy-start(f32[12,323]{1,0:T(8,128)} %param.43) | copy-start | bytes 46516
  358.0 174.0 %copy-start.24 = (f32[128,1024]{1,0:T(8,128)S(1)}, f32[128,1024]{1,0:T(8,128)}, u32[]{:S(2)}) copy-start(f32[128,1024]{1,0:T(8,128)} %get-tuple-element.83) | copy-start | bytes 1572868
  532.9 216.9 %copy-start.21 = (f32[64,2048]{1,0:T(8,128)S(1)}, f32[64,2048]{1,0:T(8,128)}, u32[]{:S(2)}) copy-start(f32[64,2048]{1,0:T(8,128)} %param.36) | copy-start | bytes 1572868
  532.9 216.9 %copy-start.43 = (f32[64,2048]{1,0:T(8,128)S(1)}, f32[64,2048]{1,0:T(8,128)}, u32[]{:S(2)}) copy-start(f32[64,2048]{1,0:T(8,128)} %param.38) | copy-start | bytes 1572868
  532.9 216.9 %copy-start.44 = (f32[64,2048]{1,0:T(8,128)S(1)}, f32[64,2048]{1,0:T(8,128)}, u32[]{:S(2)}) copy-start(f32[64,2048]{1,0:T(8,128)} %param.37) | copy-start | bytes 1572868
  644.1 204.8 %copy-start.25 = (f32[64,1920]{1,0:T(8,128)S(1)}, f32[64,1920]{1,0:T(8,128)}, u32[]{:S(2)}) copy-start(f32[64,1920]{1,0:T(8,128)} %param.27) | copy-start | bytes 1474564
  644.1 204.8 %copy-start.50 = (f32[64,1920]{1,0:T(8,128)S(1)}, f32[64,1920]{1,0:T(8,128)}, u32[]{:S(2)}) copy-start(f32[64,1920]{1,0:T(8,128)} %param.29) | copy-start | bytes 1474564
  644.1 204.8 %copy-start.51 = (f32[64,1920]{1,0:T(8,128)S(1)}, f32[64,1920]{1,0:T(8,128)}, u32[]{:S(2)}) copy-start(f32[64,1920]{1,0:T(8,128)} %param.28) | copy-start | bytes 1474564
  (122 other events, 1511.0 us)
Sparse Core Ops, SparseCore 0:
  10.9 52.5 all-gather.4
  66.2 40.9 all-gather.6
  110.8 24.7 reduce-scatter.9
  138.3 49.6 all-gather.8
  190.8 39.8 all-gather.10
  238.4 19.0 reduce-scatter.13
  260.4 14.5 reduce-scatter.11
  317.4 11.9 reduce-scatter.17
  335.5 131.9 all-reduce.47
  469.7 19.1 reduce-scatter.15
  492.8 73.3 reduce-scatter.25
  570.4 71.6 reduce-scatter.21
  646.1 103.6 reduce-scatter.23
  753.7 95.2 reduce-scatter.19
where the time goes:
time: 867 us; the launch traced here: 858 us
  waiting for transfers between devices  588 us (68%)
  blocking collectives  114 us (13%)
  matrix products  74.6 us (9%)
  other arithmetic  43.3 us (5%)
  local copies, waits for them, and re-layouts  21.7 us (3%)
  between operations  16.1 us (2%)
    psum x1, waiting for transfers between devices, per_device(): lax.psum((shared_grad, heads_full, scan_grad), ('dp', 'tensor'))  109 us
    reduce_scatter x1, waiting for transfers between devices, per_device(): lax.psum_scatter(hidden_grad, 'dp', scatter_dimension=0, tiled=True)  106 us
    reduce_scatter x1, waiting for transfers between devices, per_device(): lax.psum_scatter(mixer_grad, 'dp', scatter_dimension=0, tiled=True)  96.7 us
    reduce_scatter x1, waiting for transfers between devices, per_device(): lax.psum_scatter(merge_grad, 'dp', scatter_dimension=1, tiled=True)  73.9 us
    all_gather x1, waiting for transfers between devices, per_device(): lax.all_gather(lowered[2], 'dp', axis=0, tiled=True)  42.1 us
    psum x1, blocking collectives, per_device(): lax.psum((shared_grad, heads_full, scan_grad), ('dp', 'tensor'))  40.1 us
    all_gather x1, waiting for transfers between devices, per_device(): lax.all_gather(lowered[4], 'dp', axis=1, tiled=True)  37.8 us
    reduce_scatter x1, waiting for transfers between devices, per_device(): lax.psum_scatter(down_grad, 'dp', scatter_dimension=1, tiled=True)  33.2 us
  transfers between devices with their start and end apart: 14, of which 13 were waited for; matrix products, arithmetic and copies ran while one was open for 9% of the time, Pallas kernels for 0%

commit v1 on v0

--- a/solution.py
+++ b/solution.py
@@ -12,11 +12,12 @@
 HEADS_KV = 2
 HEAD_A = 64
 STEP = 10
+CORES = 2
 
 
 EPS = 1e-05
 THETA = 10000.0
-HIGH = lax.Precision.HIGHEST
+HIGH = lax.Precision.DEFAULT
 
 
 def scaled_norm(values, gain):
@@ -117,9 +118,13 @@
     )
 
 
-def back_dot(grad, weight):
+def dot(left, right):
+    return jnp.dot(left, right, preferred_element_type=jnp.float32)
+
+
+def dot_t(left, right):
     return lax.dot_general(
-        grad, weight, (((1,), (1,)), ((), ())), preferred_element_type=jnp.float32
+        left, right, (((1,), (1,)), ((), ())), preferred_element_type=jnp.float32
     )
 
 
@@ -130,6 +135,87 @@
     fixed_two = second / (1.0 - 0.95**STEP)
     weight = weight - rate * (fixed_one / (jnp.sqrt(fixed_two) + 1e-08) + decay * weight)
     return (first, second, weight)
+
+
+def to_own(values, chips, core):
+    split = values.reshape(values.shape[0], chips, CORES, -1)
+    zero = split[:, :, 0, :].reshape(values.shape[0], -1)
+    one = split[:, :, 1, :].reshape(values.shape[0], -1)
+    return jnp.concatenate(
+        [jnp.where(core == 0, zero, one), jnp.where(core == 0, one, zero)], axis=1
+    )
+
+
+def from_own(values, chips, core):
+    half = values.shape[1] // CORES
+    own, other = values[:, :half], values[:, half:]
+    zero = jnp.where(core == 0, own, other).reshape(values.shape[0], chips, 1, -1)
+    one = jnp.where(core == 0, other, own).reshape(values.shape[0], chips, 1, -1)
+    return jnp.concatenate([zero, one], axis=2).reshape(values.shape[0], -1)
+
+
+def swap(values, axis, distance):
+    count = lax.axis_size(axis)
+    return lax.ppermute(values, axis, [(i, i ^ distance) for i in range(count)])
+
+
+def pair_rows(own, other, tidx):
+    return jnp.where(
+        tidx == 0,
+        jnp.concatenate([own, other], axis=0),
+        jnp.concatenate([other, own], axis=0),
+    )
+
+
+def gather_rows(own, tidx):
+    return pair_rows(own, swap(own, "tensor", 1), tidx)
+
+
+def scatter_rows(partial, tidx):
+    rows = partial.shape[0] // 2
+    upper, lower = partial[:rows], partial[rows:]
+    mine = jnp.where(tidx == 0, upper, lower)
+    theirs = jnp.where(tidx == 0, lower, upper).astype(jnp.bfloat16)
+    return mine + swap(theirs, "tensor", 1).astype(jnp.float32)
+
+
+def gather_weight(shard, groups):
+    own = lax.all_gather(shard, "dp", axis=0, tiled=True, axis_index_groups=groups)
+    return own, swap(own, "dp", 1)
+
+
+def into_model(values, weight):
+    own, other = weight
+    return jnp.concatenate([dot_t(values, own), dot_t(values, other)], axis=1)
+
+
+def from_model(values, weight):
+    own, other = weight
+    half = own.shape[0]
+    return dot(values[:, :half], own) + dot(values[:, half:], other)
+
+
+def both_cores(model_side, inner_side):
+    half = model_side.shape[1] // CORES
+    model = jnp.concatenate([model_side[:, :half], swap(model_side[:, half:], "dp", 1)], axis=0)
+    inner = jnp.concatenate([inner_side, swap(inner_side, "dp", 1)], axis=0)
+    return model, inner
+
+
+def weight_grad(model_side, inner_side, groups):
+    model, inner = both_cores(model_side, inner_side)
+    grad = cross(model, inner).astype(jnp.bfloat16)
+    return lax.psum_scatter(
+        grad, "dp", scatter_dimension=0, axis_index_groups=groups, tiled=True
+    ).astype(jnp.float32)
+
+
+def sum_all(values, axis):
+    distance = 1
+    while distance < lax.axis_size(axis):
+        values = values + swap(values, axis, distance)
+        distance *= 2
+    return values
 
 
 def per_device(
@@ -158,121 +244,91 @@
     shared_first,
     shared_second,
 ):
+    low = jnp.bfloat16
     tidx = lax.axis_index("tensor")
+    count = lax.axis_size("dp")
+    chips = count // CORES
+    core = lax.axis_index("dp") % CORES
+    groups = [[i * CORES + c for i in range(chips)] for c in range(CORES)]
     group = residual.shape[0] * lax.axis_size("tensor")
     seg, pos = doc_index(doc_lengths[0], group)
-    gain_one = shared_params[:D]
-    gain_two = shared_params[D : 2 * D]
     conv_shared = shared_params[2 * D :].reshape(CONV + 1, 2 * STATE)
-    lowered = (
-        mixer_weight.astype(jnp.bfloat16),
-        scan_weight.astype(jnp.bfloat16),
-        hidden_weight.astype(jnp.bfloat16),
-        merge_weight.astype(jnp.bfloat16),
-        down_weight.astype(jnp.bfloat16),
-    )
-    mix_full, scan_full, hidden_full, merge_full, down_full = (
-        lax.all_gather(lowered[0], "dp", axis=0, tiled=True),
-        lax.all_gather(lowered[1], "dp", axis=0, tiled=True),
-        lax.all_gather(lowered[2], "dp", axis=0, tiled=True),
-        lax.all_gather(lowered[3], "dp", axis=1, tiled=True),
-        lax.all_gather(lowered[4], "dp", axis=1, tiled=True),
-    )
-    normed_one, norm_back_one = jax.vjp(scaled_norm, residual, gain_one)
-    first_in = normed_one.astype(jnp.bfloat16)
-    scan_own = jnp.dot(first_in, scan_full, preferred_element_type=jnp.float32).astype(jnp.bfloat16)
-    first_all, scan_all = (
-        lax.all_gather(first_in, "tensor", axis=0, tiled=True),
-        lax.all_gather(scan_own, "tensor", axis=0, tiled=True),
-    )
-    projected = jnp.dot(first_all, mix_full, preferred_element_type=jnp.float32).astype(
-        jnp.bfloat16
-    )
+
+    first_shard = jnp.concatenate([mixer_weight.astype(low), scan_weight.astype(low)], axis=1)
+    mix_cols = mixer_weight.shape[1]
+    first_w = gather_weight(first_shard, groups)
+    merge_w = gather_weight(merge_weight.astype(low).T, groups)
+    hidden_w = gather_weight(hidden_weight.astype(low), groups)
+    down_w = gather_weight(down_weight.astype(low).T, groups)
+    mix_w = (first_w[0][:, :mix_cols], first_w[1][:, :mix_cols])
+    scan_w = (first_w[0][:, mix_cols:], first_w[1][:, mix_cols:])
+
+    gains = to_own(shared_params[: 2 * D].reshape(2, D), chips, core)
+    resid = to_own(residual, chips, core)
+    cotangent = to_own(out_grad, chips, core)
+
+    normed_one, norm_back_one = jax.vjp(scaled_norm, resid, gains[0])
+    first_all = gather_rows(normed_one.astype(low), tidx)
+    grad_feed = gather_rows(cotangent.astype(low), tidx)
+    projected = from_model(first_all, mix_w).astype(low)
+    scan_all = from_model(first_all, scan_w).astype(low)
 
     def mixer_local(pmat, scan, heads, conv):
         return mixer(pmat, scan, heads, conv, seg, pos, tidx)
 
-    proj_wide = projected.astype(jnp.float32)
-    scan_wide = scan_all.astype(jnp.float32)
-    joined, mixer_back = jax.vjp(mixer_local, proj_wide, scan_wide, head_params, conv_shared)
-    joined_low = joined.astype(jnp.bfloat16)
-    merged = lax.psum_scatter(
-        jnp.dot(joined_low, merge_full, preferred_element_type=jnp.float32),
-        "tensor",
-        scatter_dimension=0,
-        tiled=True,
-    )
-    middle = residual + merged
-    normed_two, norm_back_two = jax.vjp(scaled_norm, middle, gain_two)
-    second_in = normed_two.astype(jnp.bfloat16)
-    second_all = lax.all_gather(second_in, "tensor", axis=0, tiled=True)
-    gate_up = jnp.dot(second_all, hidden_full, preferred_element_type=jnp.float32)
+    joined, mixer_back = jax.vjp(
+        mixer_local,
+        projected.astype(jnp.float32),
+        scan_all.astype(jnp.float32),
+        head_params,
+        conv_shared,
+    )
+    joined_low = joined.astype(low)
+    middle = resid + scatter_rows(into_model(joined_low, merge_w), tidx)
+    normed_two, norm_back_two = jax.vjp(scaled_norm, middle, gains[1])
+    second_all = gather_rows(normed_two.astype(low), tidx)
+    gate_up = from_model(second_all, hidden_w)
     units = gate_up.shape[1] // 2
     activ, swiglu_back = jax.vjp(swiglu, gate_up[:, :units], gate_up[:, units:])
-    activ_low = activ.astype(jnp.bfloat16)
-    feed = lax.psum_scatter(
-        jnp.dot(activ_low, down_full, preferred_element_type=jnp.float32).astype(jnp.bfloat16),
-        "tensor",
-        scatter_dimension=0,
-        tiled=True,
-    ).astype(jnp.float32)
-    block_out = middle + feed
-    back_mix, back_scan, back_hidden, back_merge, back_down = (
-        lax.all_gather(lowered[0], "dp", axis=0, tiled=True),
-        lax.all_gather(lowered[1], "dp", axis=0, tiled=True),
-        lax.all_gather(lowered[2], "dp", axis=0, tiled=True),
-        lax.all_gather(lowered[3], "dp", axis=1, tiled=True),
-        lax.all_gather(lowered[4], "dp", axis=1, tiled=True),
-    )
-    grad_feed = lax.all_gather(out_grad.astype(jnp.bfloat16), "tensor", axis=0, tiled=True)
-    down_grad = cross(activ_low, grad_feed)
-    grad_activ = back_dot(grad_feed, back_down)
+    activ_low = activ.astype(low)
+    block_own = middle + scatter_rows(into_model(activ_low, down_w), tidx)
+    block_out = from_own(block_own, chips, core)
+
+    down_sum = weight_grad(grad_feed, activ_low, groups).T
+    grad_activ = from_model(grad_feed, down_w)
     grad_gate, grad_upper = swiglu_back(grad_activ)
-    grad_gu = jnp.concatenate([grad_gate, grad_upper], axis=1).astype(jnp.bfloat16)
-    hidden_grad = cross(second_all, grad_gu)
-    grad_second = lax.psum_scatter(
-        back_dot(grad_gu, back_hidden), "tensor", scatter_dimension=0, tiled=True
-    )
+    grad_gu = jnp.concatenate([grad_gate, grad_upper], axis=1).astype(low)
+    hidden_sum = weight_grad(second_all, grad_gu, groups)
+    grad_second = scatter_rows(into_model(grad_gu, hidden_w), tidx)
     grad_middle_part, gain_two_grad = norm_back_two(grad_second)
-    grad_middle = out_grad + grad_middle_part
-    grad_mixed = lax.all_gather(grad_middle.astype(jnp.bfloat16), "tensor", axis=0, tiled=True)
-    merge_grad = cross(joined_low, grad_mixed)
-    grad_joined = back_dot(grad_mixed, back_merge)
+    grad_middle = cotangent + grad_middle_part
+    grad_mixed = gather_rows(grad_middle.astype(low), tidx)
+    merge_sum = weight_grad(grad_mixed, joined_low, groups).T
+    grad_joined = from_model(grad_mixed, merge_w)
     grad_proj, grad_scan, head_grad, conv_grad = mixer_back(grad_joined)
-    grad_proj_low = grad_proj.astype(jnp.bfloat16)
-    mixer_grad = cross(first_all, grad_proj_low)
-    grad_first_part, grad_scan_own = (
-        lax.psum_scatter(
-            back_dot(grad_proj_low, back_mix), "tensor", scatter_dimension=0, tiled=True
-        ),
-        lax.psum_scatter(grad_scan, "tensor", scatter_dimension=0, tiled=True),
-    )
-    grad_scan_low = grad_scan_own.astype(jnp.bfloat16)
-    scan_grad = cross(first_in, grad_scan_low)
-    grad_first = grad_first_part + back_dot(grad_scan_low, back_scan)
+    grad_proj_low = grad_proj.astype(low)
+    grad_scan_part = grad_scan.astype(low)
+    grad_scan_low = (grad_scan + swap(grad_scan_part, "tensor", 1).astype(jnp.float32)).astype(low)
+    first_sum = weight_grad(
+        first_all, jnp.concatenate([grad_proj_low, grad_scan_low], axis=1), groups
+    )
+    mixer_sum, scan_sum = first_sum[:, :mix_cols], first_sum[:, mix_cols:]
+    grad_first = scatter_rows(
+        into_model(grad_proj_low, mix_w) + into_model(grad_scan_part, scan_w), tidx
+    )
     grad_resid_part, gain_one_grad = norm_back_one(grad_first)
-    input_grad = grad_middle + grad_resid_part
-    mixer_sum, hidden_sum, merge_sum, down_sum = (
-        lax.psum_scatter(mixer_grad, "dp", scatter_dimension=0, tiled=True),
-        lax.psum_scatter(hidden_grad, "dp", scatter_dimension=0, tiled=True),
-        lax.psum_scatter(merge_grad, "dp", scatter_dimension=1, tiled=True),
-        lax.psum_scatter(down_grad, "dp", scatter_dimension=1, tiled=True),
-    )
-    head_rows = head_grad.shape[0]
-    heads_full = lax.dynamic_update_slice_in_dim(
-        jnp.zeros((HEADS_M, head_grad.shape[1]), jnp.float32), head_grad, tidx * head_rows, 0
-    )
-    shared_grad = jnp.concatenate([gain_one_grad, gain_two_grad, conv_grad.reshape(-1)])
-    shared_sum, heads_sum, scan_sum = lax.psum(
-        (shared_grad, heads_full, scan_grad), ("dp", "tensor")
-    )
-    head_sum = lax.dynamic_slice_in_dim(heads_sum, tidx * head_rows, head_rows, 0)
-    scan_rows = scan_weight.shape[0]
-    scan_own_grad = lax.dynamic_slice_in_dim(
-        scan_sum, lax.axis_index("dp") * scan_rows, scan_rows, 0
-    )
+    input_grad = from_own(grad_middle + grad_resid_part, chips, core)
+
+    gain_grads = from_own(jnp.stack([gain_one_grad, gain_two_grad]), chips, core)
+    shared_part = jnp.concatenate([gain_grads.reshape(-1), conv_grad.reshape(-1)])
+    small = jnp.concatenate([shared_part, head_grad.reshape(-1)])
+    small = sum_all(small, "dp")
+    split = shared_part.shape[0]
+    shared_sum = sum_all(small[:split], "tensor")
+    head_sum = small[split:].reshape(head_grad.shape)
+
     mixer_new = adamw(mixer_weight, mixer_first, mixer_second, mixer_sum, 0.02, 0.1)
-    scan_new = adamw(scan_weight, scan_first, scan_second, scan_own_grad, 0.02, 0.1)
+    scan_new = adamw(scan_weight, scan_first, scan_second, scan_sum, 0.02, 0.1)
     merge_new = adamw(merge_weight, merge_first, merge_second, merge_sum, 0.02, 0.1)
     hidden_new = adamw(hidden_weight, hidden_first, hidden_second, hidden_sum, 0.02, 0.1)
     down_new = adamw(down_weight, down_first, down_second, down_sum, 0.02, 0.1)
@@ -281,27 +337,13 @@
     return (
         block_out,
         input_grad,
-        mixer_new[0],
-        mixer_new[1],
-        mixer_new[2],
-        scan_new[0],
-        scan_new[1],
-        scan_new[2],
-        merge_new[0],
-        merge_new[1],
-        merge_new[2],
-        hidden_new[0],
-        hidden_new[1],
-        hidden_new[2],
-        down_new[0],
-        down_new[1],
-        down_new[2],
-        head_new[0],
-        head_new[1],
-        head_new[2],
-        shared_new[0],
-        shared_new[1],
-        shared_new[2],
+        *mixer_new,
+        *scan_new,
+        *merge_new,
+        *hidden_new,
+        *down_new,
+        *head_new,
+        *shared_new,
     )
 
 

time: 867 us -> 567 us (0.65)
  waiting for transfers between devices: 588 us -> 365 us
  blocking collectives: 114 us -> 0 us
  local copies, waits for them, and re-layouts: 21.7 us -> 39.7 us
  starting transfers between devices: 0.83 us -> 18.8 us
  other arithmetic: 43.3 us -> 52.1 us
    reduce_scatter x9 -> x4, waiting for transfers between devices: 373 us -> 157 us  [weight_grad(): lax.psum_scatter(grad, 'dp', scatter_dimension=0, axis_index_groups=group...]
    psum x1 -> x0, waiting for transfers between devices: 109 us -> none  [per_device(): lax.psum((shared_grad, heads_full, scan_grad), ('dp', 'tensor'))]
    all_gather x6 -> x0, blocking collectives: 74.2 us -> none  [the longest x1 26.3 us: per_device(): lax.all_gather(lowered[1], 'dp', axis=0, tiled=True)]
    all_gather x4, waiting for transfers between devices: 105 us -> 167 us  [gather_weight(): lax.all_gather(shard, 'dp', axis=0, tiled=True, axis_index_groups=groups)]
    ppermute x0 -> x26, waiting for transfers between devices: none -> 40.5 us  [swap(): return lax.ppermute(values, axis, [(i, i ^ distance) for i in range(count)])]
    psum x1 -> x0, blocking collectives: 40.1 us -> none  [per_device(): lax.psum((shared_grad, heads_full, scan_grad), ('dp', 'tensor'))]
    ppermute x0 -> x26, starting transfers between devices: none -> 18.2 us  [swap(): return lax.ppermute(values, axis, [(i, i ^ distance) for i in range(count)])]
    dot_general x5 -> x4, matrix products: 18.1 us -> 14.3 us  [cross(): lax.dot_general(left, right, (((0,), (0,)), ((), ())), preferred_element_...]
  transfers between devices with their start and end apart: 14 -> 34, of which waited for: 13 -> 18; matrix products, arithmetic and copies ran while one was open for 9% -> 26% of each run, Pallas kernels for 0% -> 0%
where the time goes in v1:
time: 567 us; the launch traced here: 558 us
  waiting for transfers between devices  365 us (64%)
  matrix products  66 us (12%)
  other arithmetic  52.1 us (9%)
  local copies, waits for them, and re-layouts  39.7 us (7%)
  starting transfers between devices  18.8 us (3%)
  between operations  17 us (3%)
    all_gather x4, waiting for transfers between devices, gather_weight(): lax.all_gather(shard, 'dp', axis=0, tiled=True, axis_index_groups=groups)  167 us
    reduce_scatter x4, waiting for transfers between devices, weight_grad(): lax.psum_scatter(grad, 'dp', scatter_dimension=0, axis_index_groups=group...  157 us
    ppermute x26, waiting for transfers between devices, swap(): return lax.ppermute(values, axis, [(i, i ^ distance) for i in range(count)])  40.5 us
    ppermute x26, starting transfers between devices, swap(): return lax.ppermute(values, axis, [(i, i ^ distance) for i in range(count)])  18.2 us
    dot_general x10, matrix products, dot_t(): lax.dot_general(left, right, (((1,), (1,)), ((), ())), preferred_element_...  14.5 us
    dot_general x4, matrix products, cross(): lax.dot_general(left, right, (((0,), (0,)), ((), ())), preferred_element_...  14.3 us
    dot_general x10, matrix products, dot(): return jnp.dot(left, right, preferred_element_type=jnp.float32)  14.2 us
  transfers between devices with their start and end apart: 34, of which 18 were waited for; matrix products, arithmetic and copies ran while one was open for 26% of the time, Pallas kernels for 0%

profile of v1, /device:TPU:0, one launch (start us, length us, event | category | flops | bytes accessed | tf_op | source)
XLA Modules:
  0.0 558.4 jit_solution(4045279107057417797)
XLA Ops:
  15.7 3.0 collective-permute-start
  20.4 45.4 %all-gather.5.cloned.1.call-done = bf16[512,2200]{1,0:T(8,128)(2,1)} async-done(((bf16[64,2200]{1,0:T(8,128)(2,1)}), bf16[512,2200]{1,0:T(8,128)(2,1)}) %all-gather.5.cloned.1.call-update) | async-done | bytes 2252816 | tf_op jit(solution)/shard_map/all_gather | solution.py:183
  65.7 4.3 copy.282
  77.5 29.7 %all-gather.7.cloned.1.call-done = bf16[512,1024]{1,0:T(8,128)(2,1)} async-done(((bf16[64,1024]{1,0:T(8,128)(2,1)}), bf16[512,1024]{1,0:T(8,128)(2,1)}) %all-gather.7.cloned.1.call-update) | async-done | bytes 1048592 | tf_op jit(solution)/shard_map/all_gather | solution.py:183
  107.2 41.6 %all-gather.11.cloned.1.call-done = bf16[512,1024]{1,0:T(8,128)(2,1)} async-done(((bf16[64,1024]{1,0:T(8,128)(2,1)}), bf16[512,1024]{1,0:T(8,128)(2,1)}) %all-gather.11.cloned.1.call-update) | async-done | bytes 1048592 | tf_op jit(solution)/shard_map/all_gather | solution.py:183
  148.8 50.6 %all-gather.9.cloned.1.call-done = bf16[512,2048]{1,0:T(8,128)(2,1)} async-done(((bf16[64,2048]{1,0:T(8,128)(2,1)}), bf16[512,2048]{1,0:T(8,128)(2,1)}) %all-gather.9.cloned.1.call-update) | async-done | bytes 2097168 | tf_op jit(solution)/shard_map/all_gather | solution.py:183
  199.5 2.3 fusion.21
  217.4 2.2 multiply_convert_fusion.2
  225.3 5.5 collective-permute-done.3
  233.5 5.6 %collective-permute-done.4 = bf16[128,1024]{1,0:T(8,128)(2,1)S(1)} collective-permute-done((bf16[128,1024]{1,0:T(8,128)(2,1)S(1)}, bf16[128,1024]{1,0:T(8,128)(2,1)S(1)}, u32[]{:S(2)}, u32[]{:S(2)}) %collective-permute-start.4) | collective-permute-done | bytes 262176 | tf_op jit(solution)/shard_map/ppermute | solution.py:159
  239.3 2.5 fusion.186
  244.6 2.3 fusion.195
  250.9 3.3 collective-permute-done.9
  256.4 4.1 collective-permute-done.7
  265.1 3.0 collective-permute-done.10
  270.9 3.1 fusion.18
  275.2 2.7 convolution_convert_fusion.2
  278.0 2.9 fusion.65
  282.8 3.4 reduce-window.31
  298.7 2.9 fusion.199
  301.7 3.1 convolution_convert_fusion.3
  305.1 5.1 multiply_add_fusion
  318.8 4.3 convolution_convert_fusion.1
  347.8 4.2 convolution_convert_fusion
  353.1 2.3 fusion.19
  358.0 7.6 %collective-permute-done.11 = bf16[128,1024]{1,0:T(8,128)(2,1)S(1)} collective-permute-done((bf16[128,1024]{1,0:T(8,128)(2,1)S(1)}, bf16[128,1024]{1,0:T(8,128)(2,1)S(1)}, u32[]{:S(2)}, u32[]{:S(2)}) %collective-permute-start.11) | collective-permute-done | bytes 262176 | tf_op jit(solution)/shard_map/ppermute | solution.py:159
  368.1 3.5 collective-permute-done.22
  381.7 2.5 collective-permute-done.25
  386.7 19.4 %reduce-scatter.7.cloned.1.call-done = bf16[64,1024]{1,0:T(8,128)(2,1)} async-done(((bf16[512,1024]{1,0:T(8,128)(2,1)}), bf16[64,1024]{1,0:T(8,128)(2,1)}) %reduce-scatter.7.cloned.1.call-update) | async-done | bytes 131088 | tf_op jit(solution)/shard_map/reduce_scatter | solution.py:208
  408.1 68.3 %reduce-scatter.9.cloned.1.call-done = bf16[64,2048]{1,0:T(8,128)(2,1)} async-done(((bf16[512,2048]{1,0:T(8,128)(2,1)}), bf16[64,2048]{1,0:T(8,128)(2,1)}) %reduce-scatter.9.cloned.1.call-update) | async-done | bytes 262160 | tf_op jit(solution)/shard_map/reduce_scatter | solution.py:208
  476.4 2.3 multiply_subtract_fusion
  478.8 69.2 %reduce-scatter.5.cloned.1.call-done = bf16[64,2200]{1,0:T(8,128)(2,1)} async-done(((bf16[512,2200]{1,0:T(8,128)(2,1)}), bf16[64,2200]{1,0:T(8,128)(2,1)}) %reduce-scatter.5.cloned.1.call-update) | async-done | bytes 281616 | tf_op jit(solution)/shard_map/reduce_scatter | solution.py:208
  (577 shorter events, 129.2 us)
Async XLA Ops:
  7.2 58.5 %all-gather.5.cloned.1.call-start = ((), (), s32[]{:S(2)}) async-start(), calls=%async_computation.4 | async-start | bytes 2654208 | tf_op jit(solution)/shard_map/all_gather | solution.py:183
  10.1 97.1 %all-gather.7.cloned.1.call-start = ((), (), s32[]{:S(2)}) async-start(), calls=%async_computation.5 | async-start | bytes 1179648 | tf_op jit(solution)/shard_map/all_gather | solution.py:183
  11.8 137.0 %all-gather.11.cloned.1.call-start = ((), (), s32[]{:S(2)}) async-start(), calls=%async_computation.7 | async-start | bytes 1179648 | tf_op jit(solution)/shard_map/all_gather | solution.py:183
  12.5 186.9 %all-gather.9.cloned.1.call-start = ((), (), s32[]{:S(2)}) async-start(), calls=%async_computation.6 | async-start | bytes 2359296 | tf_op jit(solution)/shard_map/all_gather | solution.py:183
  13.4 371.4 %reduce-scatter.11.cloned.1.call-start = ((), (), s32[]{:S(2)}) async-start(), calls=%async_computation.11 | async-start | bytes 1179648 | tf_op jit(solution)/shard_map/reduce_scatter | solution.py:208
  15.7 60.8 %collective-permute-start = (bf16[128,1024]{1,0:T(8,128)(2,1)S(1)}, bf16[128,1024]{1,0:T(8,128)(2,1)S(1)}, u32[]{:S(2)}, u32[]{:S(2)}) collective-permute-start(bf16[128,1024]{1,0:T(8,128)(2,1)S(1)} %multiply_convert_fusion.4), channel_id=1, source_target_pairs={{0,1},{1,0},{2,3},{3,2},{4,5},{5,4},{6,7},{7,6},{8,9},{9,8},{10,11... | collective-permute-start | bytes 786440 | tf_op jit(solution)/shard_map/ppermute | solution.py:159
  19.2 55.7 %collective-permute-start.8 = (bf16[128,1024]{1,0:T(8,128)(2,1)S(1)}, bf16[128,1024]{1,0:T(8,128)(2,1)S(1)}, u32[]{:S(2)}, u32[]{:S(2)}) collective-permute-start(bf16[128,1024]{1,0:T(8,128)(2,1)S(1)} %fusion.108), channel_id=1, source_target_pairs={{0,1},{1,0},{2,3},{3,2},{4,5},{5,4},{6,7},{7,6},{8,9},{9,8},{10,11... | collective-permute-start | bytes 786440 | tf_op jit(solution)/shard_map/ppermute | solution.py:159
  70.0 129.4 %collective-permute-start.1 = (bf16[512,2200]{0,1:T(8,128)(2,1)}, bf16[512,2200]{0,1:T(8,128)(2,1)}, u32[]{:S(2)}, u32[]{:S(2)}) collective-permute-start(bf16[512,2200]{0,1:T(8,128)(2,1)} %copy.282), channel_id=1, source_target_pairs={{0,2},{2,0},{4,6},{6,4},{8,10},{10,8},{12,14},{14,12},{16,18},{18,... | collective-permute-start | bytes 6758408 | tf_op jit(solution)/shard_map/ppermute | solution.py:159
  76.0 198.7 %collective-permute-start.19 = (bf16[256,512]{1,0:T(8,128)(2,1)}, bf16[256,512]{1,0:T(8,128)(2,1)}, u32[]{:S(2)}, u32[]{:S(2)}) collective-permute-start(bf16[256,512]{1,0:T(8,128)(2,1)} %get-tuple-element.221), channel_id=1, source_target_pairs={{0,2},{2,0},{4,6},{6,4},{8,10},{10,8},{12,14},{14,12},{16,18},{18,... | collective-permute-start | bytes 786440 | tf_op jit(solution)/shard_map/ppermute | solution.py:159
  77.4 270.4 %collective-permute-start.12 = (bf16[256,512]{1,0:T(8,128)(2,1)}, bf16[256,512]{1,0:T(8,128)(2,1)}, u32[]{:S(2)}, u32[]{:S(2)}) collective-permute-start(bf16[256,512]{1,0:T(8,128)(2,1)} %get-tuple-element.227), channel_id=1, source_target_pairs={{0,2},{2,0},{4,6},{6,4},{8,10},{10,8},{12,14},{14,12},{16,18},{18,... | collective-permute-start | bytes 786440 | tf_op jit(solution)/shard_map/ppermute | solution.py:159
  107.2 113.0 %collective-permute-start.2 = (bf16[512,1024]{1,0:T(8,128)(2,1)}, bf16[512,1024]{1,0:T(8,128)(2,1)}, u32[]{:S(2)}, u32[]{:S(2)}) collective-permute-start(bf16[512,1024]{1,0:T(8,128)(2,1)} %all-gather.7.cloned.1.call-done), channel_id=1, source_target_pairs={{0,2},{2,0},{4,6},{6,4},{8,10},{10,8},{12,14},{14,12},{16,18},{18,... | collective-permute-start | bytes 3145736 | tf_op jit(solution)/shard_map/ppermute | solution.py:159
  148.8 74.8 %collective-permute-start.6 = (bf16[512,1024]{1,0:T(8,128)(2,1)}, bf16[512,1024]{1,0:T(8,128)(2,1)}, u32[]{:S(2)}, u32[]{:S(2)}) collective-permute-start(bf16[512,1024]{1,0:T(8,128)(2,1)} %all-gather.11.cloned.1.call-done), channel_id=1, source_target_pairs={{0,2},{2,0},{4,6},{6,4},{8,10},{10,8},{12,14},{14,12},{16,18},{18,... | collective-permute-start | bytes 3145736 | tf_op jit(solution)/shard_map/ppermute | solution.py:159
  199.5 39.8 %collective-permute-start.5 = (bf16[512,2048]{1,0:T(8,128)(2,1)}, bf16[512,2048]{1,0:T(8,128)(2,1)}, u32[]{:S(2)}, u32[]{:S(2)}) collective-permute-start(bf16[512,2048]{1,0:T(8,128)(2,1)} %all-gather.9.cloned.1.call-done), channel_id=1, source_target_pairs={{0,2},{2,0},{4,6},{6,4},{8,10},{10,8},{12,14},{14,12},{16,18},{18,... | collective-permute-start | bytes 6291464 | tf_op jit(solution)/shard_map/ppermute | solution.py:159
  222.0 8.8 %collective-permute-start.3 = (bf16[128,1024]{1,0:T(8,128)(2,1)S(1)}, bf16[128,1024]{1,0:T(8,128)(2,1)S(1)}, u32[]{:S(2)}, u32[]{:S(2)}) collective-permute-start(bf16[128,1024]{1,0:T(8,128)(2,1)S(1)} %select_convert_fusion.3), channel_id=1, source_target_pairs={{0,1},{1,0},{2,3},{3,2},{4,5},{5,4},{6,7},{7,6},{8,9},{9,8},{10,11... | collective-permute-start | bytes 786440 | tf_op jit(solution)/shard_map/ppermute | solution.py:159
  231.2 8.0 %collective-permute-start.4 = (bf16[128,1024]{1,0:T(8,128)(2,1)S(1)}, bf16[128,1024]{1,0:T(8,128)(2,1)S(1)}, u32[]{:S(2)}, u32[]{:S(2)}) collective-permute-start(bf16[128,1024]{1,0:T(8,128)(2,1)S(1)} %multiply_convert_fusion.3), channel_id=1, source_target_pairs={{0,1},{1,0},{2,3},{3,2},{4,5},{5,4},{6,7},{7,6},{8,9},{9,8},{10,11... | collective-permute-start | bytes 786440 | tf_op jit(solution)/shard_map/ppermute | solution.py:159
  233.5 68.1 %collective-permute-start.16 = (bf16[256,1024]{0,1:T(8,128)(2,1)}, bf16[256,1024]{0,1:T(8,128)(2,1)}, u32[]{:S(2)}, u32[]{:S(2)}) collective-permute-start(bf16[256,1024]{0,1:T(8,128)(2,1)} %pad_maximum_fusion.6), channel_id=1, source_target_pairs={{0,2},{2,0},{4,6},{6,4},{8,10},{10,8},{12,14},{14,12},{16,18},{18,... | collective-permute-start | bytes 1572872 | tf_op jit(solution)/shard_map/ppermute | solution.py:159
  247.1 7.1 %collective-permute-start.9 = (bf16[128,1024]{1,0:T(8,128)(2,1)S(1)}, bf16[128,1024]{1,0:T(8,128)(2,1)S(1)}, u32[]{:S(2)}, u32[]{:S(2)}) collective-permute-start(bf16[128,1024]{1,0:T(8,128)(2,1)S(1)} %select_convert_fusion.1), channel_id=1, source_target_pairs={{0,1},{1,0},{2,3},{3,2},{4,5},{5,4},{6,7},{7,6},{8,9},{9,8},{10,11... | collective-permute-start | bytes 786440 | tf_op jit(solution)/shard_map/ppermute | solution.py:159
  248.6 26.6 %collective-permute-start.20 = (bf16[256,1024]{1,0:T(8,128)(2,1)S(1)}, bf16[256,1024]{1,0:T(8,128)(2,1)S(1)}, u32[]{:S(2)}, u32[]{:S(2)}) collective-permute-start(bf16[256,1024]{1,0:T(8,128)(2,1)S(1)} %get-tuple-element.211), channel_id=1, source_target_pairs={{0,2},{2,0},{4,6},{6,4},{8,10},{10,8},{12,14},{14,12},{16,18},{18,... | collective-permute-start | bytes 1572872 | tf_op jit(solution)/shard_map/ppermute | solution.py:159
  254.2 6.4 %collective-permute-start.7 = (bf16[128,1024]{1,0:T(8,128)(2,1)S(1)}, bf16[128,1024]{1,0:T(8,128)(2,1)S(1)}, u32[]{:S(2)}, u32[]{:S(2)}) collective-permute-start(bf16[128,1024]{1,0:T(8,128)(2,1)S(1)} %select_convert_fusion.2), channel_id=1, source_target_pairs={{0,1},{1,0},{2,3},{3,2},{4,5},{5,4},{6,7},{7,6},{8,9},{9,8},{10,11... | collective-permute-start | bytes 786440 | tf_op jit(solution)/shard_map/ppermute | solution.py:159
  261.7 6.4 %collective-permute-start.10 = (bf16[128,1024]{1,0:T(8,128)(2,1)S(1)}, bf16[128,1024]{1,0:T(8,128)(2,1)S(1)}, u32[]{:S(2)}, u32[]{:S(2)}) collective-permute-start(bf16[128,1024]{1,0:T(8,128)(2,1)S(1)} %get-tuple-element.198), channel_id=1, source_target_pairs={{0,1},{1,0},{2,3},{3,2},{4,5},{5,4},{6,7},{7,6},{8,9},{9,8},{10,11... | collective-permute-start | bytes 786440 | tf_op jit(solution)/shard_map/ppermute | solution.py:159
  268.1 50.7 %collective-permute-start.18 = (bf16[256,2048]{1,0:T(8,128)(2,1)}, bf16[256,2048]{1,0:T(8,128)(2,1)}, u32[]{:S(2)}, u32[]{:S(2)}) collective-permute-start(bf16[256,2048]{1,0:T(8,128)(2,1)} %pad_maximum_fusion.1), channel_id=1, source_target_pairs={{0,2},{2,0},{4,6},{6,4},{8,10},{10,8},{12,14},{14,12},{16,18},{18,... | collective-permute-start | bytes 3145736 | tf_op jit(solution)/shard_map/ppermute | solution.py:159
  274.7 44.1 %collective-permute-start.17 = (bf16[256,512]{1,0:T(8,128)(2,1)}, bf16[256,512]{1,0:T(8,128)(2,1)}, u32[]{:S(2)}, u32[]{:S(2)}) collective-permute-start(bf16[256,512]{1,0:T(8,128)(2,1)} %get-tuple-element.223), channel_id=1, source_target_pairs={{0,2},{2,0},{4,6},{6,4},{8,10},{10,8},{12,14},{14,12},{16,18},{18,... | collective-permute-start | bytes 786440 | tf_op jit(solution)/shard_map/ppermute | solution.py:159
  277.9 128.3 %reduce-scatter.7.cloned.1.call-start = ((), (), s32[]{:S(2)}) async-start(), calls=%async_computation.9 | async-start | bytes 1179648 | tf_op jit(solution)/shard_map/reduce_scatter | solution.py:208
  288.8 12.8 %collective-permute-start.15 = (bf16[256,512]{1,0:T(8,128)(2,1)}, bf16[256,512]{1,0:T(8,128)(2,1)}, u32[]{:S(2)}, u32[]{:S(2)}) collective-permute-start(bf16[256,512]{1,0:T(8,128)(2,1)} %get-tuple-element.225), channel_id=1, source_target_pairs={{0,2},{2,0},{4,6},{6,4},{8,10},{10,8},{12,14},{14,12},{16,18},{18,... | collective-permute-start | bytes 786440 | tf_op jit(solution)/shard_map/ppermute | solution.py:159
  304.8 171.6 %reduce-scatter.9.cloned.1.call-start = ((), (), s32[]{:S(2)}) async-start(), calls=%async_computation.10 | async-start | bytes 2359296 | tf_op jit(solution)/shard_map/reduce_scatter | solution.py:208
  315.3 16.3 %collective-permute-start.13 = (bf16[256,280]{0,1:T(8,128)(2,1)S(1)}, bf16[256,280]{0,1:T(8,128)(2,1)}, u32[]{:S(2)}, u32[]{:S(2)}) collective-permute-start(bf16[256,280]{0,1:T(8,128)(2,1)S(1)} %convert_element_type.146), channel_id=1, source_target_pairs={{0,1},{1,0},{2,3},{3,2},{4,5},{5,4},{6,7},{7,6},{8,9},{9,8},{10,11... | collective-permute-start | bytes 430088 | tf_op jit(solution)/shard_map/ppermute | solution.py:159
  323.1 224.8 %reduce-scatter.5.cloned.1.call-start = ((), (), s32[]{:S(2)}) async-start(), calls=%async_computation.8 | async-start | bytes 2654208 | tf_op jit(solution)/shard_map/reduce_scatter | solution.py:208
  334.5 13.4 %collective-permute-start.14 = (bf16[256,2200]{0,1:T(8,128)(2,1)}, bf16[256,2200]{0,1:T(8,128)(2,1)}, u32[]{:S(2)}, u32[]{:S(2)}) collective-permute-start(bf16[256,2200]{0,1:T(8,128)(2,1)} %pad_maximum_fusion), channel_id=1, source_target_pairs={{0,2},{2,0},{4,6},{6,4},{8,10},{10,8},{12,14},{14,12},{16,18},{18,... | collective-permute-start | bytes 3379208 | tf_op jit(solution)/shard_map/ppermute | solution.py:159
  357.1 8.6 %collective-permute-start.11 = (bf16[128,1024]{1,0:T(8,128)(2,1)S(1)}, bf16[128,1024]{1,0:T(8,128)(2,1)S(1)}, u32[]{:S(2)}, u32[]{:S(2)}) collective-permute-start(bf16[128,1024]{1,0:T(8,128)(2,1)S(1)} %select_convert_fusion), channel_id=1, source_target_pairs={{0,1},{1,0},{2,3},{3,2},{4,5},{5,4},{6,7},{7,6},{8,9},{9,8},{10,11... | collective-permute-start | bytes 786440 | tf_op jit(solution)/shard_map/ppermute | solution.py:159
  367.5 4.1 collective-permute-start.22
  371.6 3.9 collective-permute-start.23
  375.5 4.8 collective-permute-start.24
  (160 other events, 4025.6 us)
Sparse Core Ops, SparseCore 0:
  10.8 54.8 all-gather.4
  68.4 38.6 all-gather.6
  109.9 38.8 all-gather.10
  151.4 48.0 all-gather.8
  278.0 61.9 reduce-scatter.10
  343.7 62.4 reduce-scatter.6
  409.7 66.6 reduce-scatter.8
  479.9 67.9 reduce-scatter.4

commit v2 on v1

--- a/solution.py
+++ b/solution.py
@@ -1,6 +1,8 @@
 import jax
 import jax.numpy as jnp
 from jax import lax
+from jax.experimental import pallas as pl
+from jax.experimental.pallas import tpu as pltpu
 from jax.sharding import PartitionSpec as P
 
 D = 1024
@@ -179,9 +181,129 @@
     return mine + swap(theirs, "tensor", 1).astype(jnp.float32)
 
 
-def gather_weight(shard, groups):
-    own = lax.all_gather(shard, "dp", axis=0, tiled=True, axis_index_groups=groups)
-    return own, swap(own, "dp", 1)
+RING_CHIPS = 8
+
+
+def ring_chip(place):
+    place = place % RING_CHIPS
+    half = RING_CHIPS // 2
+    if isinstance(place, int):
+        return 2 * place if place < half else 2 * (RING_CHIPS - 1 - place) + 1
+    return jnp.where(place < half, 2 * place, 2 * (RING_CHIPS - 1 - place) + 1)
+
+
+def ring_place(chip):
+    return jnp.where(chip % 2 == 0, chip // 2, RING_CHIPS - 1 - chip // 2)
+
+
+def ring_step(values, way):
+    pairs = [
+        (CORES * ring_chip(p) + c, CORES * ring_chip(p + way) + c)
+        for p in range(RING_CHIPS)
+        for c in range(CORES)
+    ]
+    return lax.ppermute(values, "dp", pairs)
+
+
+def place_pieces(pieces, offsets, columns, rows):
+    count = len(pieces)
+    height, low = pieces[0].shape[0], pieces[0].dtype
+
+    def kernel(offset_ref, *refs):
+        out_ref, sem = refs[count], refs[count + 1]
+        copies = []
+        for i in range(count):
+            start = pl.multiple_of(offset_ref[i] * height, height)
+            copies.append(
+                pltpu.make_async_copy(
+                    refs[i],
+                    out_ref.at[pl.ds(start, height), pl.ds(columns[i], pieces[i].shape[1])],
+                    sem.at[i],
+                )
+            )
+        for copy in copies:
+            copy.start()
+        for copy in copies:
+            copy.wait()
+
+    width = max(c + p.shape[1] for c, p in zip(columns, pieces))
+    return pl.pallas_call(
+        kernel,
+        out_shape=jax.ShapeDtypeStruct((rows, width), low),
+        in_specs=[pl.BlockSpec(memory_space=pltpu.SMEM)]
+        + [pl.BlockSpec(memory_space=pl.ANY)] * count,
+        out_specs=pl.BlockSpec(memory_space=pl.ANY),
+        scratch_shapes=[pltpu.SemaphoreType.DMA((count,))],
+        name="place_pieces",
+    )(offsets, *pieces)
+
+
+def ring_gather(shard, cuts, place):
+    pieces, offsets, columns, marks = [], [], [], []
+    chains = [[shard[:, a:b]] for a, b, _ in cuts]
+    for step in range(1, RING_CHIPS):
+        for chain, (_, _, way) in zip(chains, cuts):
+            chain.append(ring_step(chain[-1], way))
+        marks.append(chains[0][-1])
+    for chain, (a, _, way) in zip(chains, cuts):
+        for step, piece in enumerate(chain):
+            pieces.append(piece)
+            offsets.append(ring_chip(place - way * step))
+            columns.append(a)
+    own = place_pieces(
+        pieces, jnp.stack(offsets).astype(jnp.int32), columns, RING_CHIPS * shard.shape[0]
+    )
+    return (own, swap(own, "dp", 1)), marks
+
+
+def ring_reduce(grad, cuts, place):
+    rows = grad.shape[0] // RING_CHIPS
+
+    def local(chip, a, b):
+        return lax.dynamic_slice(grad, (chip * rows, a), (rows, b - a))
+
+    sums = [None] * len(cuts)
+    for step in range(1, RING_CHIPS + 1):
+        for i, (a, b, way) in enumerate(cuts):
+            part = local(ring_chip(place - way * step), a, b)
+            if step > 1:
+                part = part + sums[i].astype(jnp.float32)
+            if step < RING_CHIPS:
+                part = ring_step(part.astype(jnp.bfloat16), way)
+            sums[i] = part
+    return jnp.concatenate(sums, axis=1)
+
+
+def after(values, mark):
+    return lax.optimization_barrier((values, mark))[0]
+
+
+def halves(width):
+    return ((0, width // 2, 1), (width // 2, width, -1))
+
+
+def quarters(width):
+    cut = [width * i // 4 // 128 * 128 for i in range(4)] + [width]
+    return tuple((cut[i], cut[i + 1], 1 if i % 2 == 0 else -1) for i in range(4))
+
+
+def gather_weights(first, merge, hidden, down, chips, place):
+    if chips == RING_CHIPS:
+        first_w, marks = ring_gather(first, quarters(first.shape[1]), place)
+        merge_w, _ = ring_gather(after(merge, marks[4]), halves(merge.shape[1]), place)
+        hidden_w, more = ring_gather(after(hidden, marks[6]), halves(hidden.shape[1]), place)
+        down_w, _ = ring_gather(after(down, more[4]), halves(down.shape[1]), place)
+        return first_w, merge_w, hidden_w, down_w
+    groups = core_groups(chips)
+    full = []
+    for shard in (first, merge, hidden, down):
+        own = lax.all_gather(shard, "dp", axis=0, tiled=True, axis_index_groups=groups)
+        full.append((own, swap(own, "dp", 1)))
+    return tuple(full)
+
+
+def core_groups(chips):
+    return [[i * CORES + c for i in range(chips)] for c in range(CORES)]
 
 
 def into_model(values, weight):
@@ -202,11 +324,17 @@
     return model, inner
 
 
-def weight_grad(model_side, inner_side, groups):
+def weight_grad(model_side, inner_side, chips, place, cut):
     model, inner = both_cores(model_side, inner_side)
-    grad = cross(model, inner).astype(jnp.bfloat16)
+    grad = cross(model, inner)
+    if chips == RING_CHIPS:
+        return ring_reduce(grad, cut(grad.shape[1]), place)
     return lax.psum_scatter(
-        grad, "dp", scatter_dimension=0, axis_index_groups=groups, tiled=True
+        grad.astype(jnp.bfloat16),
+        "dp",
+        scatter_dimension=0,
+        axis_index_groups=core_groups(chips),
+        tiled=True,
     ).astype(jnp.float32)
 
 
@@ -249,19 +377,28 @@
     count = lax.axis_size("dp")
     chips = count // CORES
     core = lax.axis_index("dp") % CORES
-    groups = [[i * CORES + c for i in range(chips)] for c in range(CORES)]
+    place = ring_place(lax.axis_index("dp") // CORES)
     group = residual.shape[0] * lax.axis_size("tensor")
     seg, pos = doc_index(doc_lengths[0], group)
     conv_shared = shared_params[2 * D :].reshape(CONV + 1, 2 * STATE)
 
-    first_shard = jnp.concatenate([mixer_weight.astype(low), scan_weight.astype(low)], axis=1)
     mix_cols = mixer_weight.shape[1]
-    first_w = gather_weight(first_shard, groups)
-    merge_w = gather_weight(merge_weight.astype(low).T, groups)
-    hidden_w = gather_weight(hidden_weight.astype(low), groups)
-    down_w = gather_weight(down_weight.astype(low).T, groups)
+    scan_cols = scan_weight.shape[1]
+    both_cols = mix_cols + scan_cols
+    spare = jnp.zeros((mixer_weight.shape[0], -both_cols % 256), low)
+    first_shard = jnp.concatenate(
+        [mixer_weight.astype(low), scan_weight.astype(low), spare], axis=1
+    )
+    first_w, merge_w, hidden_w, down_w = gather_weights(
+        first_shard,
+        merge_weight.astype(low).T,
+        hidden_weight.astype(low),
+        down_weight.astype(low).T,
+        chips,
+        place,
+    )
     mix_w = (first_w[0][:, :mix_cols], first_w[1][:, :mix_cols])
-    scan_w = (first_w[0][:, mix_cols:], first_w[1][:, mix_cols:])
+    scan_w = (first_w[0][:, mix_cols:both_cols], first_w[1][:, mix_cols:both_cols])
 
     gains = to_own(shared_params[: 2 * D].reshape(2, D), chips, core)
     resid = to_own(residual, chips, core)
@@ -294,25 +431,31 @@
     block_own = middle + scatter_rows(into_model(activ_low, down_w), tidx)
     block_out = from_own(block_own, chips, core)
 
-    down_sum = weight_grad(grad_feed, activ_low, groups).T
+    down_sum = weight_grad(grad_feed, activ_low, chips, place, halves).T
     grad_activ = from_model(grad_feed, down_w)
     grad_gate, grad_upper = swiglu_back(grad_activ)
     grad_gu = jnp.concatenate([grad_gate, grad_upper], axis=1).astype(low)
-    hidden_sum = weight_grad(second_all, grad_gu, groups)
+    hidden_sum = weight_grad(second_all, grad_gu, chips, place, halves)
     grad_second = scatter_rows(into_model(grad_gu, hidden_w), tidx)
     grad_middle_part, gain_two_grad = norm_back_two(grad_second)
     grad_middle = cotangent + grad_middle_part
     grad_mixed = gather_rows(grad_middle.astype(low), tidx)
-    merge_sum = weight_grad(grad_mixed, joined_low, groups).T
+    merge_sum = weight_grad(grad_mixed, joined_low, chips, place, halves).T
     grad_joined = from_model(grad_mixed, merge_w)
     grad_proj, grad_scan, head_grad, conv_grad = mixer_back(grad_joined)
     grad_proj_low = grad_proj.astype(low)
     grad_scan_part = grad_scan.astype(low)
     grad_scan_low = (grad_scan + swap(grad_scan_part, "tensor", 1).astype(jnp.float32)).astype(low)
     first_sum = weight_grad(
-        first_all, jnp.concatenate([grad_proj_low, grad_scan_low], axis=1), groups
-    )
-    mixer_sum, scan_sum = first_sum[:, :mix_cols], first_sum[:, mix_cols:]
+        first_all,
+        jnp.concatenate(
+            [grad_proj_low, grad_scan_low, jnp.zeros((group, spare.shape[1]), low)], axis=1
+        ),
+        chips,
+        place,
+        quarters,
+    )
+    mixer_sum, scan_sum = first_sum[:, :mix_cols], first_sum[:, mix_cols:both_cols]
     grad_first = scatter_rows(
         into_model(grad_proj_low, mix_w) + into_model(grad_scan_part, scan_w), tidx
     )

time: 567 us -> 702 us (1.24)
  waiting for transfers between devices: 365 us -> 139 us
  Pallas kernels: 0 us -> 206 us
  starting transfers between devices: 18.8 us -> 171 us
  other arithmetic: 52.1 us -> 65.7 us
  between operations: 17 us -> 5.08 us
    pallas_call x0 -> x4, Pallas kernels: none -> 206 us  [place_pieces(): pl.pallas_call(kernel, out_shape=jax.ShapeDtypeStruct((rows, width), low)...]
    all_gather x4 -> x0, waiting for transfers between devices: 167 us -> none  [gather_weight(): lax.all_gather(shard, 'dp', axis=0, tiled=True, axis_index_groups=groups)]
    reduce_scatter x4 -> x0, waiting for transfers between devices: 157 us -> none  [weight_grad(): lax.psum_scatter(grad, 'dp', scatter_dimension=0, axis_index_groups=group...]
    ppermute x0 -> x140, starting transfers between devices: none -> 154 us  [ring_step(): return lax.ppermute(values, 'dp', pairs)]
    ppermute x0 -> x140, waiting for transfers between devices: none -> 108 us  [ring_step(): return lax.ppermute(values, 'dp', pairs)]
    convert_element_type x2 -> x56, other arithmetic: 1.73 us -> 14.2 us  [the longest x55 14.1 us: ring_reduce(): part = ring_step(part.astype(jnp.bfloat16), way)]
    ppermute x26, waiting for transfers between devices: 40.5 us -> 31.5 us  [swap(): return lax.ppermute(values, axis, [(i, i ^ distance) for i in range(count)])]
  transfers between devices with their start and end apart: 34 -> 166, of which waited for: 18 -> 74; matrix products, arithmetic and copies ran while one was open for 26% -> 23% of each run, Pallas kernels for 0% -> 30%
where the time goes in v2:
time: 702 us; the launch traced here: 692 us
  Pallas kernels  206 us (29%)
  starting transfers between devices  171 us (24%)
  waiting for transfers between devices  139 us (20%)
  matrix products  66.2 us (9%)
  other arithmetic  65.7 us (9%)
  local copies, waits for them, and re-layouts  38.4 us (5%)
    pallas_call x4, Pallas kernels, place_pieces(): pl.pallas_call(kernel, out_shape=jax.ShapeDtypeStruct((rows, width), low)...  206 us
    ppermute x140, starting transfers between devices, ring_step(): return lax.ppermute(values, 'dp', pairs)  154 us
    ppermute x140, waiting for transfers between devices, ring_step(): return lax.ppermute(values, 'dp', pairs)  108 us
    ppermute x26, waiting for transfers between devices, swap(): return lax.ppermute(values, axis, [(i, i ^ distance) for i in range(count)])  31.5 us
    ppermute x26, starting transfers between devices, swap(): return lax.ppermute(values, axis, [(i, i ^ distance) for i in range(count)])  17.5 us
    dot_general x10, matrix products, dot(): return jnp.dot(left, right, preferred_element_type=jnp.float32)  16.6 us
    dot_general x10, matrix products, dot_t(): lax.dot_general(left, right, (((1,), (1,)), ((), ())), preferred_element_...  16.1 us
    dot_general x3, matrix products, mixer(): jnp.einsum('hts,shp->thp', decay * inner[None], weighted, precision=HIGH)  15.8 us
  transfers between devices with their start and end apart: 166, of which 74 were waited for; matrix products, arithmetic and copies ran while one was open for 23% of the time, Pallas kernels for 30%

profile of v2, /device:TPU:0, one launch (start us, length us, event | category | flops | bytes accessed | tf_op | source)
XLA Modules:
  0.0 692.3 jit_solution(16526905083343007104)
XLA Ops:
  1.8 3.1 collective-permute-start.1
  13.2 2.7 collective-permute-done.2.refs_2_
  17.5 3.1 collective-permute-done.3.refs_3_
  58.5 73.5 %place_pieces.4 = bf16[512,2304]{1,0:T(8,128)(2,1)} custom-call(s32[32]{0:T(128)} %stack.51.offset_ref, bf16[64,512]{1,0:T(8,128)(2,1)} %copy-done.66, bf16[64,512]{1,0:T(8,128)(2,1)} %copy-done.115, bf16[64,512]{1,0:T(8,128)(2,1)} %copy-done.116, bf16[64,512]{1,0:T(8,128)(2,1)} %copy-done.117, bf16[64,512]{1,0:T(8,128)(2,1)} %copy-done.118, ...), custom_call_target="tpu_custom_call" | custom-call | tf_op jit(solution)/shard_map/place_pieces/pallas_call | solution.py:230
  150.8 2.5 collective-permute-done.54.refs_9_
  196.2 33.7 %place_pieces.5 = bf16[512,1024]{1,0:T(8,128)(2,1)} custom-call(s32[16]{0:T(128)} %stack.52.offset_ref, bf16[64,512]{1,0:T(8,128)(2,1)} %copy-done.74, bf16[64,512]{1,0:T(8,128)(2,1)} %copy-done.128, bf16[64,512]{1,0:T(8,128)(2,1)} %copy-done.130, bf16[64,512]{1,0:T(8,128)(2,1)} %copy-done.132, bf16[64,512]{1,0:T(8,128)(2,1)} %copy-done.134, ...), custom_call_target="tpu_custom_call" | custom-call | tf_op jit(solution)/shard_map/place_pieces/pallas_call | solution.py:230
  230.8 65.4 %place_pieces.6 = bf16[512,2048]{1,0:T(8,128)(2,1)} custom-call(s32[16]{0:T(128)} %stack.52.offset_ref, bf16[64,1024]{1,0:T(8,128)(2,1)} %copy-done.51, bf16[64,1024]{1,0:T(8,128)(2,1)} %copy-done.83, bf16[64,1024]{1,0:T(8,128)(2,1)} %copy-done.84, bf16[64,1024]{1,0:T(8,128)(2,1)} %copy-done.85, bf16[64,1024]{1,0:T(8,128)(2,1)} %copy-done.86, ...), custom_call_target="tpu_custom_call" | custom-call | tf_op jit(solution)/shard_map/place_pieces/pallas_call | solution.py:230
  297.5 33.7 %place_pieces.7 = bf16[512,1024]{1,0:T(8,128)(2,1)} custom-call(s32[16]{0:T(128)} %stack.52.offset_ref, bf16[64,512]{1,0:T(8,128)(2,1)} %copy-done.76, bf16[64,512]{1,0:T(8,128)(2,1)} %copy-done.135, bf16[64,512]{1,0:T(8,128)(2,1)} %copy-done.140, bf16[64,512]{1,0:T(8,128)(2,1)} %copy-done.143, bf16[64,512]{1,0:T(8,128)(2,1)} %copy-done.147, ...), custom_call_target="tpu_custom_call" | custom-call | tf_op jit(solution)/shard_map/place_pieces/pallas_call | solution.py:230
  331.3 2.6 fusion.25
  358.5 5.8 collective-permute-done.45
  367.4 5.2 collective-permute-done.46
  388.5 4.3 collective-permute-done.79
  394.8 5.7 collective-permute-done.77
  414.4 4.5 collective-permute-done.80
  423.0 11.0 %fusion.22 = (f32[12,256]{1,0:T(8,128)S(1)}, f32[12,256]{1,0:T(8,128)S(1)}, bf16[256,256]{1,0:T(8,128)(2,1)S(1)}) fusion(f32[256,256]{1,0:T(8,128)S(1)} %copy-done.72, f32[12,256]{1,0:T(8,128)S(1)} %bitcast.245, pred[256,256]{1,0:T(8,128)(4,1)S(1)} %copy-done.161, f32[256,12,64]{0,2,1:T(8,128)S(1)} %bitcast.220, f32[256,12]{0,1:T(8,128)S(1)} %copy-done.163, ...), kind=kOutput, calls=%fused_computation.26 | convolution fusion | flops 110422016 | bytes 2867200 | tf_op jit(solution)/shard_map/transpose(jvp(hts,shp->thp))/dot_general | solution.py:96
  441.1 2.7 multiply_add_fusion
  443.9 2.5 reduce-window.31
  455.1 4.8 multiply_reduce_fusion.5
  476.2 3.4 collective-permute-done.148
  526.3 2.5 collective-permute-done.116
  538.2 3.6 collective-permute-done.155
  545.8 2.9 fusion.15
  557.6 3.5 collective-permute-done.157
  562.5 3.3 collective-permute-done.120
  567.4 2.8 collective-permute-done.158
  576.3 3.1 collective-permute-done.159
  585.8 4.2 collective-permute-done.124
  601.2 2.7 collective-permute-done.127
  606.3 2.6 collective-permute-done.128
  608.9 2.7 collective-permute-done.135
  613.0 3.7 collective-permute-done.136
  681.6 3.7 collective-permute-done.111
  (1049 shorter events, 375.6 us)
Async XLA Ops:
  6.6 140.4 %collective-permute-start.78 = (bf16[128,1024]{1,0:T(8,128)(2,1)S(1)}, bf16[128,1024]{1,0:T(8,128)(2,1)S(1)}, u32[]{:S(2)}, u32[]{:S(2)}) collective-permute-start(bf16[128,1024]{1,0:T(8,128)(2,1)S(1)} %fusion.113), channel_id=1, source_target_pairs={{0,1},{1,0},{2,3},{3,2},{4,5},{5,4},{6,7},{7,6},{8,9},{9,8},{10,11... | collective-permute-start | bytes 786440 | tf_op jit(solution)/shard_map/ppermute | solution.py:161
  8.2 15.0 %collective-permute-start.15 = (bf16[64,512]{1,0:T(8,128)(2,1)S(1)}, bf16[64,512]{1,0:T(8,128)(2,1)}, u32[]{:S(2)}, u32[]{:S(2)}) collective-permute-start(bf16[64,512]{1,0:T(8,128)(2,1)S(1)} %get-tuple-element.249.refs_16_), channel_id=1, source_target_pairs={{0,8},{2,10},{8,16},{10,18},{16,24},{18,26},{24,28},{26,30},{28,20... | collective-permute-start | bytes 196616 | tf_op jit(solution)/shard_map/ppermute | solution.py:205
  9.9 14.9 %collective-permute-start.22 = (bf16[64,640]{1,0:T(8,128)(2,1)S(1)}, bf16[64,640]{1,0:T(8,128)(2,1)S(1)}, u32[]{:S(2)}, u32[]{:S(2)}) collective-permute-start(bf16[64,640]{1,0:T(8,128)(2,1)S(1)} %slice.398.refs_24_), channel_id=1, source_target_pairs={{0,4},{2,6},{8,0},{10,2},{16,8},{18,10},{24,16},{26,18},{28,24},{3... | collective-permute-start | bytes 245768 | tf_op jit(solution)/shard_map/ppermute | solution.py:205
  10.4 14.9 %collective-permute-start.8 = (bf16[64,640]{1,0:T(8,128)(2,1)S(1)}, bf16[64,640]{1,0:T(8,128)(2,1)S(1)}, u32[]{:S(2)}, u32[]{:S(2)}) collective-permute-start(bf16[64,640]{1,0:T(8,128)(2,1)S(1)} %slice.396.refs_8_), channel_id=1, source_target_pairs={{0,4},{2,6},{8,0},{10,2},{16,8},{18,10},{24,16},{26,18},{28,24},{3... | collective-permute-start | bytes 245768 | tf_op jit(solution)/shard_map/ppermute | solution.py:205
  52.8 81.5 %collective-permute-start.49 = (bf16[64,1024]{1,0:T(8,128)(2,1)S(1)}, bf16[64,1024]{1,0:T(8,128)(2,1)S(1)}, u32[]{:S(2)}, u32[]{:S(2)}) collective-permute-start(bf16[64,1024]{1,0:T(8,128)(2,1)S(1)} %collective-permute-done.48.refs_2_), channel_id=1, source_target_pairs={{0,8},{2,10},{8,16},{10,18},{16,24},{18,26},{24,28},{26,30},{28,20... | collective-permute-start | bytes 393224 | tf_op jit(solution)/shard_map/ppermute | solution.py:205
  55.2 77.0 %collective-permute-start.30 = (bf16[64,512]{1,0:T(8,128)(2,1)S(1)}, bf16[64,512]{1,0:T(8,128)(2,1)S(1)}, u32[]{:S(2)}, u32[]{:S(2)}) collective-permute-start(bf16[64,512]{1,0:T(8,128)(2,1)S(1)} %get-tuple-element.254.refs_0_), channel_id=1, source_target_pairs={{0,8},{2,10},{8,16},{10,18},{16,24},{18,26},{24,28},{26,30},{28,20... | collective-permute-start | bytes 196616 | tf_op jit(solution)/shard_map/ppermute | solution.py:205
  56.9 76.8 %collective-permute-start.37 = (bf16[64,512]{1,0:T(8,128)(2,1)S(1)}, bf16[64,512]{1,0:T(8,128)(2,1)S(1)}, u32[]{:S(2)}, u32[]{:S(2)}) collective-permute-start(bf16[64,512]{1,0:T(8,128)(2,1)S(1)} %get-tuple-element.253.refs_8_), channel_id=1, source_target_pairs={{0,4},{2,6},{8,0},{10,2},{16,8},{18,10},{24,16},{26,18},{28,24},{3... | collective-permute-start | bytes 196616 | tf_op jit(solution)/shard_map/ppermute | solution.py:205
  132.1 199.1 %collective-permute-start.29 = (bf16[512,2304]{1,0:T(8,128)(2,1)}, bf16[512,2304]{1,0:T(8,128)(2,1)}, u32[]{:S(2)}, u32[]{:S(2)}) collective-permute-start(bf16[512,2304]{1,0:T(8,128)(2,1)} %place_pieces.4), channel_id=1, source_target_pairs={{0,2},{2,0},{4,6},{6,4},{8,10},{10,8},{12,14},{14,12},{16,18},{18,... | collective-permute-start | bytes 7077896 | tf_op jit(solution)/shard_map/ppermute | solution.py:161
  142.3 13.0 %collective-permute-start = (bf16[128,1024]{1,0:T(8,128)(2,1)S(1)}, bf16[128,1024]{1,0:T(8,128)(2,1)S(1)}, u32[]{:S(2)}, u32[]{:S(2)}) collective-permute-start(bf16[128,1024]{1,0:T(8,128)(2,1)S(1)} %multiply_convert_fusion.4), channel_id=1, source_target_pairs={{0,1},{1,0},{2,3},{3,2},{4,5},{5,4},{6,7},{7,6},{8,9},{9,8},{10,11... | collective-permute-start | bytes 786440 | tf_op jit(solution)/shard_map/ppermute | solution.py:161
  164.7 13.2 %collective-permute-start.36 = (bf16[64,512]{1,0:T(8,128)(2,1)S(1)}, bf16[64,512]{1,0:T(8,128)(2,1)}, u32[]{:S(2)}, u32[]{:S(2)}) collective-permute-start(bf16[64,512]{1,0:T(8,128)(2,1)S(1)} %collective-permute-done.35.refs_6_), channel_id=1, source_target_pairs={{0,8},{2,10},{8,16},{10,18},{16,24},{18,26},{24,28},{26,30},{28,20... | collective-permute-start | bytes 196616 | tf_op jit(solution)/shard_map/ppermute | solution.py:205
  190.8 39.3 %collective-permute-start.53 = (bf16[64,1024]{1,0:T(8,128)(2,1)S(1)}, bf16[64,1024]{1,0:T(8,128)(2,1)S(1)}, u32[]{:S(2)}, u32[]{:S(2)}) collective-permute-start(bf16[64,1024]{1,0:T(8,128)(2,1)S(1)} %collective-permute-done.52.refs_6_), channel_id=1, source_target_pairs={{0,8},{2,10},{8,16},{10,18},{16,24},{18,26},{24,28},{26,30},{28,20... | collective-permute-start | bytes 393224 | tf_op jit(solution)/shard_map/ppermute | solution.py:205
  192.0 38.1 %collective-permute-start.60 = (bf16[64,1024]{1,0:T(8,128)(2,1)S(1)}, bf16[64,1024]{1,0:T(8,128)(2,1)S(1)}, u32[]{:S(2)}, u32[]{:S(2)}) collective-permute-start(bf16[64,1024]{1,0:T(8,128)(2,1)S(1)} %collective-permute-done.59.refs_14_), channel_id=1, source_target_pairs={{0,4},{2,6},{8,0},{10,2},{16,8},{18,10},{24,16},{26,18},{28,24},{3... | collective-permute-start | bytes 393224 | tf_op jit(solution)/shard_map/ppermute | solution.py:205
  192.9 103.4 %collective-permute-start.68 = (bf16[64,512]{1,0:T(8,128)(2,1)S(1)}, bf16[64,512]{1,0:T(8,128)(2,1)S(1)}, u32[]{:S(2)}, u32[]{:S(2)}) collective-permute-start(bf16[64,512]{1,0:T(8,128)(2,1)S(1)} %collective-permute-done.67.refs_6_), channel_id=1, source_target_pairs={{0,8},{2,10},{8,16},{10,18},{16,24},{18,26},{24,28},{26,30},{28,20... | collective-permute-start | bytes 196616 | tf_op jit(solution)/shard_map/ppermute | solution.py:205
  194.1 102.8 %collective-permute-start.75 = (bf16[64,512]{1,0:T(8,128)(2,1)S(1)}, bf16[64,512]{1,0:T(8,128)(2,1)S(1)}, u32[]{:S(2)}, u32[]{:S(2)}) collective-permute-start(bf16[64,512]{1,0:T(8,128)(2,1)S(1)} %collective-permute-done.74.refs_14_), channel_id=1, source_target_pairs={{0,4},{2,6},{8,0},{10,2},{16,8},{18,10},{24,16},{26,18},{28,24},{3... | collective-permute-start | bytes 196616 | tf_op jit(solution)/shard_map/ppermute | solution.py:205
  230.0 180.0 %collective-permute-start.145 = (bf16[256,512]{1,0:T(8,128)(2,1)}, bf16[256,512]{1,0:T(8,128)(2,1)}, u32[]{:S(2)}, u32[]{:S(2)}) collective-permute-start(bf16[256,512]{1,0:T(8,128)(2,1)} %get-tuple-element.224), channel_id=1, source_target_pairs={{0,2},{2,0},{4,6},{6,4},{8,10},{10,8},{12,14},{14,12},{16,18},{18,... | collective-permute-start | bytes 786440 | tf_op jit(solution)/shard_map/ppermute | solution.py:161
  230.1 386.9 %collective-permute-start.82 = (bf16[256,512]{1,0:T(8,128)(2,1)}, bf16[256,512]{1,0:T(8,128)(2,1)}, u32[]{:S(2)}, u32[]{:S(2)}) collective-permute-start(bf16[256,512]{1,0:T(8,128)(2,1)} %get-tuple-element.230), channel_id=1, source_target_pairs={{0,2},{2,0},{4,6},{6,4},{8,10},{10,8},{12,14},{14,12},{16,18},{18,... | collective-permute-start | bytes 786440 | tf_op jit(solution)/shard_map/ppermute | solution.py:161
  296.3 57.4 %collective-permute-start.44 = (bf16[512,1024]{1,0:T(8,128)(2,1)}, bf16[512,1024]{1,0:T(8,128)(2,1)}, u32[]{:S(2)}, u32[]{:S(2)}) collective-permute-start(bf16[512,1024]{1,0:T(8,128)(2,1)} %place_pieces.5), channel_id=1, source_target_pairs={{0,2},{2,0},{4,6},{6,4},{8,10},{10,8},{12,14},{14,12},{16,18},{18,... | collective-permute-start | bytes 3145736 | tf_op jit(solution)/shard_map/ppermute | solution.py:161
  296.9 76.8 %collective-permute-start.61 = (bf16[512,2048]{1,0:T(8,128)(2,1)}, bf16[512,2048]{1,0:T(8,128)(2,1)}, u32[]{:S(2)}, u32[]{:S(2)}) collective-permute-start(bf16[512,2048]{1,0:T(8,128)(2,1)} %place_pieces.6), channel_id=1, source_target_pairs={{0,2},{2,0},{4,6},{6,4},{8,10},{10,8},{12,14},{14,12},{16,18},{18,... | collective-permute-start | bytes 6291464 | tf_op jit(solution)/shard_map/ppermute | solution.py:161
  331.2 25.7 %collective-permute-start.76 = (bf16[512,1024]{1,0:T(8,128)(2,1)}, bf16[512,1024]{1,0:T(8,128)(2,1)}, u32[]{:S(2)}, u32[]{:S(2)}) collective-permute-start(bf16[512,1024]{1,0:T(8,128)(2,1)} %place_pieces.7), channel_id=1, source_target_pairs={{0,2},{2,0},{4,6},{6,4},{8,10},{10,8},{12,14},{14,12},{16,18},{18,... | collective-permute-start | bytes 3145736 | tf_op jit(solution)/shard_map/ppermute | solution.py:161
  366.8 131.0 %collective-permute-start.114 = (bf16[256,1024]{0,1:T(8,128)(2,1)}, bf16[256,1024]{0,1:T(8,128)(2,1)}, u32[]{:S(2)}, u32[]{:S(2)}) collective-permute-start(bf16[256,1024]{0,1:T(8,128)(2,1)} %pad_maximum_fusion.6), channel_id=1, source_target_pairs={{0,2},{2,0},{4,6},{6,4},{8,10},{10,8},{12,14},{14,12},{16,18},{18,... | collective-permute-start | bytes 1572872 | tf_op jit(solution)/shard_map/ppermute | solution.py:161
  373.6 170.1 %collective-permute-start.129 = (bf16[256,512]{1,0:T(8,128)(2,1)}, bf16[256,512]{1,0:T(8,128)(2,1)}, u32[]{:S(2)}, u32[]{:S(2)}) collective-permute-start(bf16[256,512]{1,0:T(8,128)(2,1)} %get-tuple-element.226), channel_id=1, source_target_pairs={{0,2},{2,0},{4,6},{6,4},{8,10},{10,8},{12,14},{14,12},{16,18},{18,... | collective-permute-start | bytes 786440 | tf_op jit(solution)/shard_map/ppermute | solution.py:161
  414.1 60.1 %collective-permute-start.147 = (bf16[64,512]{1,0:T(8,128)(2,1)}, bf16[64,512]{1,0:T(8,128)(2,1)}, u32[]{:S(2)}, u32[]{:S(2)}) collective-permute-start(bf16[64,512]{1,0:T(8,128)(2,1)} %get-tuple-element.208), channel_id=1, source_target_pairs={{0,8},{2,10},{8,16},{10,18},{16,24},{18,26},{24,28},{26,30},{28,20... | collective-permute-start | bytes 196616 | tf_op jit(solution)/shard_map/ppermute | solution.py:205
  454.0 27.4 %collective-permute-start.83 = (bf16[256,280]{0,1:T(8,128)(2,1)S(1)}, bf16[256,280]{0,1:T(8,128)(2,1)}, u32[]{:S(2)}, u32[]{:S(2)}) collective-permute-start(bf16[256,280]{0,1:T(8,128)(2,1)S(1)} %convert_element_type.546), channel_id=1, source_target_pairs={{0,1},{1,0},{2,3},{3,2},{4,5},{5,4},{6,7},{7,6},{8,9},{9,8},{10,11... | collective-permute-start | bytes 430088 | tf_op jit(solution)/shard_map/ppermute | solution.py:161
  479.6 13.1 %collective-permute-start.81 = (bf16[128,1024]{1,0:T(8,128)(2,1)}, bf16[128,1024]{1,0:T(8,128)(2,1)S(1)}, u32[]{:S(2)}, u32[]{:S(2)}) collective-permute-start(bf16[128,1024]{1,0:T(8,128)(2,1)} %select_convert_fusion), channel_id=1, source_target_pairs={{0,1},{1,0},{2,3},{3,2},{4,5},{5,4},{6,7},{7,6},{8,9},{9,8},{10,11... | collective-permute-start | bytes 786440 | tf_op jit(solution)/shard_map/ppermute | solution.py:161
  491.1 53.7 %collective-permute-start.130 = (bf16[256,2048]{1,0:T(8,128)(2,1)}, bf16[256,2048]{1,0:T(8,128)(2,1)}, u32[]{:S(2)}, u32[]{:S(2)}) collective-permute-start(bf16[256,2048]{1,0:T(8,128)(2,1)} %pad_maximum_fusion.1), channel_id=1, source_target_pairs={{0,2},{2,0},{4,6},{6,4},{8,10},{10,8},{12,14},{14,12},{16,18},{18,... | collective-permute-start | bytes 3145736 | tf_op jit(solution)/shard_map/ppermute | solution.py:161
  510.2 20.5 %collective-permute-start.154 = (bf16[64,512]{1,0:T(8,128)(2,1)}, bf16[64,512]{1,0:T(8,128)(2,1)S(1)}, u32[]{:S(2)}, u32[]{:S(2)}) collective-permute-start(bf16[64,512]{1,0:T(8,128)(2,1)} %get-tuple-element.209), channel_id=1, source_target_pairs={{0,4},{2,6},{8,0},{10,2},{16,8},{18,10},{24,16},{26,18},{28,24},{3... | collective-permute-start | bytes 196616 | tf_op jit(solution)/shard_map/ppermute | solution.py:205
  530.8 86.3 %collective-permute-start.84 = (bf16[256,2304]{0,1:T(8,128)(2,1)}, bf16[256,2304]{0,1:T(8,128)(2,1)S(1)}, u32[]{:S(2)}, u32[]{:S(2)}) collective-permute-start(bf16[256,2304]{0,1:T(8,128)(2,1)} %pad_maximum_fusion), channel_id=1, source_target_pairs={{0,2},{2,0},{4,6},{6,4},{8,10},{10,8},{12,14},{14,12},{16,18},{18,... | collective-permute-start | bytes 3538952 | tf_op jit(solution)/shard_map/ppermute | solution.py:161
  541.8 29.4 %collective-permute-start.122 = (bf16[64,512]{1,0:T(8,128)(2,1)}, bf16[64,512]{1,0:T(8,128)(2,1)S(1)}, u32[]{:S(2)}, u32[]{:S(2)}) collective-permute-start(bf16[64,512]{1,0:T(8,128)(2,1)} %get-tuple-element.213), channel_id=1, source_target_pairs={{0,4},{2,6},{8,0},{10,2},{16,8},{18,10},{24,16},{26,18},{28,24},{3... | collective-permute-start | bytes 196616 | tf_op jit(solution)/shard_map/ppermute | solution.py:205
  554.6 72.8 %collective-permute-start.138 = (bf16[64,1024]{1,0:T(8,128)(2,1)S(1)}, bf16[64,1024]{1,0:T(8,128)(2,1)S(1)}, u32[]{:S(2)}, u32[]{:S(2)}) collective-permute-start(bf16[64,1024]{1,0:T(8,128)(2,1)S(1)} %get-tuple-element.203), channel_id=1, source_target_pairs={{0,4},{2,6},{8,0},{10,2},{16,8},{18,10},{24,16},{26,18},{28,24},{3... | collective-permute-start | bytes 393224 | tf_op jit(solution)/shard_map/ppermute | solution.py:205
  571.2 14.3 %collective-permute-start.132 = (bf16[64,1024]{1,0:T(8,128)(2,1)S(1)}, bf16[64,1024]{1,0:T(8,128)(2,1)S(1)}, u32[]{:S(2)}, u32[]{:S(2)}) collective-permute-start(bf16[64,1024]{1,0:T(8,128)(2,1)S(1)} %add_convert_fusion.13), channel_id=1, source_target_pairs={{0,8},{2,10},{8,16},{10,18},{16,24},{18,26},{24,28},{26,30},{28,20... | collective-permute-start | bytes 393224 | tf_op jit(solution)/shard_map/ppermute | solution.py:205
  619.9 30.3 %collective-permute-start.99 = (bf16[64,512]{1,0:T(8,128)(2,1)S(1)}, bf16[64,512]{1,0:T(8,128)(2,1)S(1)}, u32[]{:S(2)}, u32[]{:S(2)}) collective-permute-start(bf16[64,512]{1,0:T(8,128)(2,1)S(1)} %get-tuple-element.195), channel_id=1, source_target_pairs={{0,8},{2,10},{8,16},{10,18},{16,24},{18,26},{24,28},{26,30},{28,20... | collective-permute-start | bytes 196616 | tf_op jit(solution)/shard_map/ppermute | solution.py:205
  623.8 34.7 %collective-permute-start.106 = (bf16[64,640]{1,0:T(8,128)(2,1)S(1)}, bf16[64,640]{1,0:T(8,128)(2,1)S(1)}, u32[]{:S(2)}, u32[]{:S(2)}) collective-permute-start(bf16[64,640]{1,0:T(8,128)(2,1)S(1)} %get-tuple-element.199), channel_id=1, source_target_pairs={{0,4},{2,6},{8,0},{10,2},{16,8},{18,10},{24,16},{26,18},{28,24},{3... | collective-permute-start | bytes 245768 | tf_op jit(solution)/shard_map/ppermute | solution.py:205
  (359 other events, 5795.0 us)
